TPU v7x, 32 devices: a whole 2x2x4 slice. The times are simulated.
32 devices in a mesh: groups: 2 (over x), row: 8 (over z, y), col: 2 (over core).
Axes of the slice: x: 2, y: 2, z: 4, core: 2. Of those that a mesh axis runs over, the one named last changes fastest.
Arguments:
- tokens_in: bfloat16 [16, 256, 768], P('groups', 'row'), parts along dimension 0, may hold values from -6 to 6
- cond_single: bfloat16 [512, 768], P(('groups', 'row')), parts along dimension 0, may hold values from -6 to 6
- token_mask: int32 [512], P(('groups', 'row')), parts along dimension 0, may hold values 0 or 1
- pair_cond: bfloat16 [512, 256, 128], P(('groups', 'row'), 'col'), parts along dimension 0, may hold values from -1000 to 1000
- w_pair: bfloat16 [128, 16], replicated, may hold values from -0.5 to 0.5
- w_scale: bfloat16 [768, 768], replicated, may hold values from -0.21875 to 0.21875
- w_shift: bfloat16 [768, 768], replicated, may hold values from -0.21875 to 0.21875
- w_outgate: bfloat16 [768, 768], replicated, may hold values from -0.21875 to 0.21875
- w_query: bfloat16 [768, 768], P(None, 'col'), may hold values from -0.21875 to 0.21875
- w_key: bfloat16 [768, 768], P(None, 'col'), may hold values from -0.21875 to 0.21875
- w_value: bfloat16 [768, 768], P(None, 'col'), may hold values from -0.21875 to 0.21875
- w_gate: bfloat16 [768, 768], P(None, 'col'), may hold values from -0.21875 to 0.21875
- w_out: bfloat16 [768, 768], P('col'), may hold values from -0.21875 to 0.21875
- atom_cond: bfloat16 [4096, 128], P(('groups', 'row', 'col')), parts along dimension 0, may hold values from -6 to 6
- atom_token: int32 [4096], P(('groups', 'row', 'col')), parts along dimension 0, may hold values from 0 to 255, as said below
- window_start: int32 [128], P(('groups', 'row', 'col')), parts along dimension 0, may hold values from 0 to 1920, as said below
- atom_mask: int32 [4096], P(('groups', 'row', 'col')), parts along dimension 0, may hold values 0 or 1
- atom_pair: bfloat16 [128, 16, 32, 128], P(('groups', 'row', 'col')), parts along dimension 0, may hold values from -1000 to 1000
- w_token_atom: bfloat16 [768, 128], replicated, may hold values from -0.21875 to 0.21875
- w_ascale: bfloat16 [128, 128], replicated, may hold values from -0.5 to 0.5
- w_ashift: bfloat16 [128, 128], replicated, may hold values from -0.5 to 0.5
- w_aquery: bfloat16 [128, 128], replicated, may hold values from -0.5 to 0.5
- w_akey: bfloat16 [128, 128], replicated, may hold values from -0.5 to 0.5
- w_avalue: bfloat16 [128, 128], replicated, may hold values from -0.5 to 0.5
- w_agate: bfloat16 [128, 128], replicated, may hold values from -0.5 to 0.5
- w_aout: bfloat16 [128, 128], replicated, may hold values from -0.5 to 0.5
- w_apair: bfloat16 [16, 4], replicated, may hold values from -1.5 to 1.5
- w_update: bfloat16 [3, 128], replicated, may hold values from -0.5 to 0.5
Outputs:
- tokens_out: bfloat16 [16, 256, 768], P('groups', 'row'), parts along dimension 0
- atom_update: float32 [16, 3, 2048], P('groups', None, ('row', 'col')), parts along dimension 0
There are 2 independent parts, one for each index of `groups`. A program takes and returns all parts, laid end to end along the dimension named above; an argument that names none is the same for every part. Nothing has to cross between parts.
Inputs may be any that keep to these rules, and one draw needn't show every extreme that they name: atom_token[l] differs from l // 8 by at most 16. window_start[k] differs from k * 32 + 32 // 2 - 128 // 2 by at most 16, unless it is clipped to the range.
All inputs are finite; a program needn't handle non-finite values. No bound on the sum of `token_mask` or of `atom_mask` on one device may be relied on, other than what follows from the above.
Results may differ from a plain program's by a relative error of at most 0.0075.
Values may be sent and summed in bfloat16 or wider, within the bound.
A program may use at most 128 MiB of HBM per device.

v0:
```python
import jax
import jax.numpy as jnp
from jax import lax
from jax.sharding import PartitionSpec as P

HEAD = 48
AHEADS = 4
AHEAD = 32
WQ = 32
WK = 128


def extended_2(cells, sides, width):
    for axis, dim in sides:
        count = lax.axis_size(axis)
        ends = count - 1
        head = lax.slice_in_dim(cells, 0, width, axis=dim)
        tail = lax.slice_in_dim(cells, cells.shape[dim] - width, cells.shape[dim], axis=dim)
        cells = jnp.concatenate(
            [
                lax.ppermute(tail, axis, [(i, (i + 1) % count) for i in range(ends)]),
                cells,
                lax.ppermute(head, axis, [((i + 1) % count, i) for i in range(ends)]),
            ],
            axis=dim,
        )
    return cells


def layer_norm(inputs):
    inputs = inputs.astype(jnp.float32)
    centred = inputs - jnp.mean(inputs, axis=-1, keepdims=True)
    variance = jnp.mean(centred * centred, axis=-1, keepdims=True)
    return centred * lax.rsqrt(variance + 1e-05)


def project_rows(sample_rows, w_token_atom):
    token_norm = layer_norm(sample_rows).astype(jnp.bfloat16)
    return jnp.einsum(
        "std,de->ste", token_norm, w_token_atom, preferred_element_type=jnp.float32
    ).astype(jnp.bfloat16)


def shards(
    tokens_in,
    cond_single,
    token_mask,
    pair_cond,
    w_pair,
    w_scale,
    w_shift,
    w_outgate,
    w_query,
    w_key,
    w_value,
    w_gate,
    w_out,
    atom_cond,
    atom_token,
    window_start,
    atom_mask,
    atom_pair,
    w_token_atom,
    w_ascale,
    w_ashift,
    w_aquery,
    w_akey,
    w_avalue,
    w_agate,
    w_aout,
    w_apair,
    w_update,
):
    samples, tok_rows, feature_width = tokens_in.shape
    local_heads = w_query.shape[1] // HEAD
    inv_root = HEAD ** (-0.5)
    cond_norm = layer_norm(cond_single).astype(jnp.bfloat16)
    ada_scale = jax.nn.sigmoid(jnp.dot(cond_norm, w_scale, preferred_element_type=jnp.float32))
    ada_shift = jnp.dot(cond_norm, w_shift, preferred_element_type=jnp.float32)
    out_gate = jax.nn.sigmoid(jnp.dot(cond_norm, w_outgate, preferred_element_type=jnp.float32))
    local_bias = jnp.einsum("ijc,ch->hij", pair_cond, w_pair, preferred_element_type=jnp.float32)
    pair_bias = lax.all_to_all(local_bias, "col", split_axis=0, concat_axis=2, tiled=True)
    mixed_rows = (ada_scale[None] * layer_norm(tokens_in) + ada_shift[None]).astype(jnp.bfloat16)
    queries = (
        jnp.einsum("sqd,de->sqe", mixed_rows, w_query, preferred_element_type=jnp.float32)
        * inv_root
    ).astype(jnp.bfloat16)
    queries = queries.reshape(samples, tok_rows, local_heads, HEAD)
    key_rows = jnp.einsum(
        "sqd,de->sqe", mixed_rows, w_key, preferred_element_type=jnp.float32
    ).astype(jnp.bfloat16)
    value_rows = jnp.einsum(
        "sqd,de->sqe", mixed_rows, w_value, preferred_element_type=jnp.float32
    ).astype(jnp.bfloat16)
    head_gate = jax.nn.sigmoid(
        jnp.einsum("sqd,de->sqe", mixed_rows, w_gate, preferred_element_type=jnp.float32)
    )
    stacked = jnp.stack([key_rows, value_rows])
    mask_row = token_mask.astype(jnp.bfloat16).reshape(1, 1, tok_rows)
    row_max = jnp.full((samples, local_heads, tok_rows), -1e30, jnp.float32)
    kv_piece = lax.all_gather(stacked, "row", axis=2, tiled=True)
    mask_piece = lax.all_gather(mask_row, "row", axis=2, tiled=True)
    key_count = kv_piece.shape[2]
    piece_keys = kv_piece[0].reshape(samples, key_count, local_heads, HEAD)
    piece_values = kv_piece[1].reshape(samples, key_count, local_heads, HEAD)
    mask_shift = ((mask_piece.astype(jnp.float32) - 1.0) * 10000.0).reshape(1, 1, 1, key_count)
    scores = (
        jnp.einsum("sqhd,skhd->shqk", queries, piece_keys, preferred_element_type=jnp.float32)
        + pair_bias[None]
        + mask_shift
    )
    new_max = jnp.maximum(row_max, jnp.max(scores, axis=-1))
    weights = jnp.exp(scores - new_max[..., None])
    totals = jnp.sum(weights, axis=-1)
    summed = jnp.einsum(
        "shqk,skhd->shqd",
        weights.astype(jnp.bfloat16),
        piece_values,
        preferred_element_type=jnp.float32,
    )
    row_max, totals, summed = (new_max, totals, summed)
    attended = jnp.transpose(summed / totals[..., None], (0, 2, 1, 3)).reshape(
        samples, tok_rows, local_heads * HEAD
    )
    gated = (head_gate * attended).astype(jnp.bfloat16)
    partial_value = jnp.einsum("sqe,ed->sqd", gated, w_out, preferred_element_type=jnp.float32)
    update = lax.psum(partial_value.astype(jnp.bfloat16), "col").astype(jnp.float32)
    tokens_out = (tokens_in.astype(jnp.float32) + out_gate[None] * update).astype(jnp.bfloat16)
    projected = project_rows(tokens_out, w_token_atom)
    lookup = extended_2(projected, (("row", 1),), tok_rows // 2)
    local_token = atom_token - (lax.axis_index("row") * tok_rows - tok_rows // 2)
    atom_rows = atom_cond.shape[0]
    local_windows = atom_rows // WQ
    cond_anorm = layer_norm(atom_cond).astype(jnp.bfloat16)
    atom_scale = jax.nn.sigmoid(jnp.dot(cond_anorm, w_ascale, preferred_element_type=jnp.float32))
    atom_shift = jnp.dot(cond_anorm, w_ashift, preferred_element_type=jnp.float32)
    atom_state = atom_cond.astype(jnp.float32)[None] + jnp.take(lookup, local_token, axis=1).astype(
        jnp.float32
    )
    atom_mixed = (atom_scale[None] * layer_norm(atom_state) + atom_shift[None]).astype(jnp.bfloat16)
    atom_root = AHEAD ** (-0.5)
    atom_queries = (
        jnp.einsum("sad,de->sae", atom_mixed, w_aquery, preferred_element_type=jnp.float32)
        * atom_root
    ).astype(jnp.bfloat16)
    atom_queries = atom_queries.reshape(samples, local_windows, WQ, AHEADS, AHEAD)
    atom_gate = jax.nn.sigmoid(
        jnp.einsum("sad,de->sae", atom_mixed, w_agate, preferred_element_type=jnp.float32)
    )
    atom_keys = jnp.einsum(
        "sad,de->sae", atom_mixed, w_akey, preferred_element_type=jnp.float32
    ).astype(jnp.bfloat16)
    atom_values = jnp.einsum(
        "sad,de->sae", atom_mixed, w_avalue, preferred_element_type=jnp.float32
    ).astype(jnp.bfloat16)
    extended = extended_2(jnp.stack([atom_keys, atom_values]), ((("row", "col"), 2),), WK // 2)
    wide_keys = extended[0]
    wide_values = extended[1]
    window_offset = window_start - (lax.axis_index(("row", "col")) * atom_rows - WK // 2)
    key_index = window_offset[:, None] + jnp.arange(WK, dtype=jnp.int32)[None, :]
    window_keys = jnp.take(wide_keys, key_index, axis=1).reshape(
        samples, local_windows, WK, AHEADS, AHEAD
    )
    window_values = jnp.take(wide_values, key_index, axis=1).reshape(
        samples, local_windows, WK, AHEADS, AHEAD
    )
    atom_bias = jnp.einsum("wcqk,ch->whqk", atom_pair, w_apair, preferred_element_type=jnp.float32)
    atom_scores = (
        jnp.einsum(
            "swqhd,swkhd->swhqk", atom_queries, window_keys, preferred_element_type=jnp.float32
        )
        + atom_bias[None]
    )
    atom_max = jnp.max(atom_scores, axis=-1, keepdims=True)
    atom_weights = jnp.exp(atom_scores - atom_max)
    atom_totals = jnp.sum(atom_weights, axis=-1, keepdims=True)
    atom_attended = jnp.einsum(
        "swhqk,swkhd->swqhd",
        atom_weights.astype(jnp.bfloat16),
        window_values,
        preferred_element_type=jnp.float32,
    )
    atom_attended = atom_attended / jnp.transpose(atom_totals, (0, 1, 3, 2, 4))
    atom_gated = (atom_gate * atom_attended.reshape(samples, atom_rows, AHEADS * AHEAD)).astype(
        jnp.bfloat16
    )
    atom_final = atom_state + jnp.einsum(
        "sad,de->sae", atom_gated, w_aout, preferred_element_type=jnp.float32
    )
    final_norm = layer_norm(atom_final).astype(jnp.bfloat16)
    atom_update = jnp.einsum(
        "cd,sad->sca", w_update, final_norm, preferred_element_type=jnp.float32
    )
    atom_update = atom_update * atom_mask.astype(jnp.float32)[None, None, :]
    return (tokens_out, atom_update)


def solution(mesh):
    return jax.shard_map(
        shards,
        mesh=mesh,
        in_specs=(
            P("groups", "row", None),
            P(("groups", "row"), None),
            P(("groups", "row")),
            P(("groups", "row"), "col", None),
            P(),
            P(),
            P(),
            P(),
            P(None, "col"),
            P(None, "col"),
            P(None, "col"),
            P(None, "col"),
            P("col", None),
            P(("groups", "row", "col"), None),
            P(("groups", "row", "col")),
            P(("groups", "row", "col")),
            P(("groups", "row", "col")),
            P(("groups", "row", "col"), None, None, None),
            P(),
            P(),
            P(),
            P(),
            P(),
            P(),
            P(),
            P(),
            P(),
            P(),
        ),
        out_specs=(P("groups", "row", None), P("groups", None, ("row", "col"))),
        check_vma=False,
    )
```

profile of v0, /device:TPU:1, one launch (start us, length us, event | category | flops | bytes accessed | tf_op | source)
XLA Modules:
  0.0 169.7 jit_solution(7626165011451416089)
XLA Ops:
  10.5 1.7 %fusion.97 = f32[32,768]{1,0:T(8,128)S(1)} fusion(bf16[768,768]{1,0:T(8,128)(2,1)} %param.36, bf16[32,768]{1,0:T(8,128)(2,1)} %param.31, f32[32]{0:T(128)S(1)} %add_rsqrt_fusion.5, f32[32]{0:T(128)S(1)} %broadcast_multiply_fusion.5), kind=kOutput, calls=%fused_computation.164 | convolution fusion | flops 37847040 | bytes 1327360 | tf_op jit(solution)/shard_map/dot_general | solution.py:79
  15.7 3.6 %all-to-all-start = ((f32[16,32,128]{2,1,0:T(8,128)}), f32[16,32,128]{2,1,0:T(8,128)S(1)}, u32[]{:S(2)}, u32[]{:S(2)}) async-start(f32[16,32,128]{2,1,0:T(8,128)} %copy.68), calls=%async_computation | async-start | bytes 524288 | tf_op jit(solution)/shard_map/all_to_all | solution.py:82
  19.8 1.2 reshape.125
  21.1 1.3 dynamic-slice
  23.4 19.5 %all-reduce = bf16[256]{0:T(256)(128)(2,1)S(1)} all-reduce(bf16[256]{0:T(256)(128)(2,1)S(1)} %dynamic-update-slice), channel_id=2, replica_groups=mesh['groups'=2,'row'=8,'col'=2] {'row'}, use_global_device_ids=true, to_apply=%add | all-reduce | flops 256 | bytes 1024
  45.1 1.6 fusion.30
  48.6 28.0 %all-gather.3.cloned.1.call-done = bf16[2,8,256,384]{3,2,1,0:T(8,128)(2,1)} async-done(((bf16[2,8,32,384]{3,2,1,0:T(8,128)(2,1)}), bf16[2,8,256,384]{3,2,1,0:T(8,128)(2,1)}) %all-gather.3.cloned.1.call-update) | async-done | bytes 3145744 | tf_op jit(solution)/shard_map/all_gather | solution.py:101
  76.7 3.4 %fusion.112 = (bf16[1,8,256,384]{3,2,1,0:T(8,128)(2,1)S(1)}, bf16[1,8,256,384]{3,2,1,0:T(8,128)(2,1)}) fusion(bf16[2,8,256,384]{3,2,1,0:T(8,128)(2,1)} %all-gather.3.cloned.1.call-done), kind=kLoop, calls=%fused_computation.165 | loop fusion | bytes 6291456 | tf_op jit(solution)/shard_map/slice | solution.py:104
  80.1 1.7 copy.66
  81.8 2.0 %fusion = (f32[8,8,32]{2,1,0:T(8,128)S(1)}, f32[8,8,32,256]{3,2,1,0:T(8,128)S(1)}) fusion(f32[256]{0:T(256)} %add_multiply_fusion, f32[8,32,256]{2,1,0:T(8,128)S(1)} %bitcast.138, bf16[8,256,8,48]{1,3,2,0:T(8,128)(2,1)} %bitcast.134, bf16[8,32,8,48]{3,2,1,0:T(8,128)(2,1)} %reshape.125), kind=kOutput, calls=%fused_computation.8 | convolution fusion | flops 51902464 | bytes 4137984 | tf_op jit(solution)/shard_map/sqhd,skhd->shqk/dot_general | solution.py:108
  84.4 2.6 %copy.70 = bf16[1,8,256,384]{2,3,1,0:T(8,128)(2,1)} copy(bf16[1,8,256,384]{3,2,1,0:T(8,128)(2,1)} %get-tuple-element.14) | data formatting | bytes 3145728 | tf_op jit(solution)/shard_map/slice | solution.py:105
  87.0 1.6 fusion.3
  90.6 2.8 %convolution_convert_fusion = bf16[8,32,768]{2,1,0:T(8,128)(2,1)} fusion(f32[8,32,384]{2,1,0:T(8,128)S(1)} %reshape.127, bf16[384,768]{1,0:T(8,128)(2,1)} %param.42, bf16[768,384]{1,0:T(8,128)(2,1)} %param.41, bf16[8,32,768]{2,1,0:T(8,128)(2,1)S(1)} %copy-done.2, f32[32,768]{1,0:T(8,128)S(1)} %copy-done.19, f32[8,32]{1,0:T(8,128)S(1)} %copy-done.28, ...), kind=kOutput, calls=%fused_computation.15 | convolution fusion | flops 303857664 | bytes 2557952 | tf_op jit(solution)/shard_map/sqe,ed->sqd/dot_general | solution.py:126
  94.1 1.7 fusion.25
  95.8 16.1 %all-reduce.3.cloned.1.call-done = bf16[8,32,768]{2,1,0:T(8,128)(2,1)} async-done(((bf16[8,32,768]{2,1,0:T(8,128)(2,1)}), bf16[8,32,768]{2,1,0:T(8,128)(2,1)}) %all-reduce.3.cloned.1.call-update) | async-done | bytes 393232 | tf_op jit(solution)/shard_map/psum | solution.py:127
  111.9 1.2 convert_reduce_fusion.1
  114.2 3.4 %collective-permute-start = (bf16[8,16,128]{2,1,0:T(8,128)(2,1)S(1)}, bf16[8,16,128]{2,1,0:T(8,128)(2,1)S(1)}, u32[]{:S(2)}, u32[]{:S(2)}) collective-permute-start(bf16[8,16,128]{2,1,0:T(8,128)(2,1)S(1)} %get-tuple-element.19), channel_id=1, source_target_pairs={{0,2},{2,4},{4,6},{6,8},{8,10},{10,12},{12,14},{1,3},{3,5},{5,7},{... | collective-permute-start | bytes 98312 | tf_op jit(solution)/shard_map/ppermute | solution.py:21
  117.6 1.3 collective-permute-start.1
  119.2 3.1 %collective-permute-done.1 = bf16[8,16,128]{2,1,0:T(8,128)(2,1)S(1)} collective-permute-done((bf16[8,16,128]{2,1,0:T(8,128)(2,1)S(1)}, bf16[8,16,128]{2,1,0:T(8,128)(2,1)S(1)}, u32[]{:S(2)}, u32[]{:S(2)}) %collective-permute-start.1) | collective-permute-done | bytes 32800 | tf_op jit(solution)/shard_map/ppermute | solution.py:23
  125.1 5.5 %collective-permute-start.2 = (bf16[2,8,64,128]{3,2,1,0:T(8,128)(2,1)}, bf16[2,8,64,128]{3,2,1,0:T(8,128)(2,1)}, u32[]{:S(2)}, u32[]{:S(2)}) collective-permute-start(bf16[2,8,64,128]{3,2,1,0:T(8,128)(2,1)} %get-tuple-element.17), channel_id=1, source_target_pairs={{0,1},{1,2},{2,3},{3,4},{4,5},{5,6},{6,7},{7,8},{8,9},{9,10},{10,1... | collective-permute-start | bytes 786440 | tf_op jit(solution)/shard_map/ppermute | solution.py:21
  130.6 2.1 %collective-permute-start.3 = (bf16[2,8,64,128]{3,2,1,0:T(8,128)(2,1)S(1)}, bf16[2,8,64,128]{3,2,1,0:T(8,128)(2,1)}, u32[]{:S(2)}, u32[]{:S(2)}) collective-permute-start(bf16[2,8,64,128]{3,2,1,0:T(8,128)(2,1)S(1)} %get-tuple-element.18), channel_id=1, source_target_pairs={{1,0},{2,1},{3,2},{4,3},{5,4},{6,5},{7,6},{8,7},{9,8},{10,9},{11,1... | collective-permute-start | bytes 786440 | tf_op jit(solution)/shard_map/ppermute | solution.py:23
  134.2 4.2 %collective-permute-done.3 = bf16[2,8,64,128]{3,2,1,0:T(8,128)(2,1)} collective-permute-done((bf16[2,8,64,128]{3,2,1,0:T(8,128)(2,1)S(1)}, bf16[2,8,64,128]{3,2,1,0:T(8,128)(2,1)}, u32[]{:S(2)}, u32[]{:S(2)}) %collective-permute-start.3) | collective-permute-done | bytes 262176 | tf_op jit(solution)/shard_map/ppermute | solution.py:23
  140.3 2.4 %gather_fusion.1 = bf16[512,8,128]{2,1,0:T(8,128)(2,1)} fusion(bf16[8,256,128]{2,0,1:T(8,128)(2,1)S(1)} %copy.80, s32[1024]{0:T(1024)S(1)} %pad_clamp_fusion), kind=kCustom, calls=%fused_computation.clone | custom fusion | bytes 2099200 | tf_op jit(solution)/shard_map/jit(_take)/gather | solution.py:164
  142.7 2.4 %gather_fusion.2 = bf16[512,8,128]{2,1,0:T(8,128)(2,1)} fusion(bf16[8,256,128]{2,0,1:T(8,128)(2,1)S(1)} %copy.83, s32[1024]{0:T(1024)S(1)} %pad_clamp_fusion), kind=kCustom, calls=%fused_computation.1.clone | custom fusion | bytes 2099200 | tf_op jit(solution)/shard_map/jit(_take)/gather | solution.py:161
  145.1 2.9 %select_bitcast_fusion = (bf16[8,4,128,128]{3,0,2,1:T(8,128)(2,1)}, bf16[8,4,128,128]{3,0,2,1:T(8,128)(2,1)}) fusion(bf16[4,128,8,128]{3,2,1,0:T(8,128)(2,1)} %bitcast.136, pred[4,128]{1,0:T(4,128)(4,1)S(1)} %copy-done.34, bf16[4,128,8,128]{3,2,1,0:T(8,128)(2,1)} %bitcast.135), kind=kLoop, calls=%fused_computation.63 | loop fusion | flops 1048576 | bytes 4194816 | tf_op jit(solution)/shard_map/jit(_take)/select_n | solution.py:161
  148.0 1.7 %copy.84 = bf16[8,4,128,128]{2,3,1,0:T(8,128)(2,1)S(1)} copy(bf16[8,4,128,128]{3,0,2,1:T(8,128)(2,1)} %get-tuple-element.21) | data formatting | bytes 2097152 | tf_op jit(solution)/shard_map/jit(_take)/select_n | solution.py:161
  149.8 2.4 %copy.81 = bf16[8,4,128,128]{2,3,1,0:T(8,128)(2,1)} copy(bf16[8,4,128,128]{3,0,2,1:T(8,128)(2,1)} %get-tuple-element.22) | data formatting | bytes 2097152 | tf_op jit(solution)/shard_map/jit(_take)/select_n | solution.py:164
  153.0 1.4 fusion.1
  154.4 2.0 %bitcast_divide_fusion = f32[8,4,32,4,32]{2,4,3,1,0:T(8,128)} fusion(bf16[8,4,128,4,32]{2,4,3,1,0:T(8,128)(2,1)S(1)} %bitcast.142, f32[8,4,4,32,128]{4,3,2,1,0:T(8,128)S(1)} %get-tuple-element.26, f32[8,4,32,4]{2,3,1,0:T(4,128)S(1)} %bitcast.144, f32[8,4,4,32]{3,2,1,0:T(4,128)S(1)} %get-tuple-element.25, f32[4,4,32,128]{3,2,1,0:T(8,128)S(1)} %copy.87), kind=kOutput, calls=%fused_computation.3 | convolution fusion | flops 35258368 | bytes 3964928 | tf_op jit(solution)/shard_map/swhqk,swkhd->swqhd/dot_general | solution.py:177
  156.5 2.1 %copy.88 = f32[8,4,32,4,32]{4,3,2,1,0:T(4,128)S(1)} copy(f32[8,4,32,4,32]{2,4,3,1,0:T(8,128)} %bitcast_divide_fusion) | data formatting | bytes 1048576 | tf_op jit(solution)/shard_map/div | solution.py:183
  158.5 1.7 reshape.131
  160.2 1.7 %fusion.114 = (f32[8,128]{1,0:T(8,128)S(1)}, f32[8,128,128]{1,2,0:T(8,128)S(1)}) fusion(bf16[128,128]{1,0:T(8,128)(2,1)} %param.55, f32[8,128,128]{2,1,0:T(8,128)} %reshape.131, bf16[128,128]{1,0:T(8,128)(2,1)} %param.54, f32[128,128]{0,1:T(8,128)} %copy-done.11, f32[128,128]{0,1:T(8,128)} %fusion.96, f32[8,128]{1,0:T(8,128)S(1)} %copy-done.30, ...), kind=kOutput, calls=%fused_computation.167 | convolution fusion | flops 69467136 | bytes 1585280 | tf_op jit(solution)/shard_map/sad,de->sae/dot_general | solution.py:187
  (171 shorter events, 23.5 us)
Async XLA Ops:
  7.2 69.5 %all-gather.3.cloned.1.call-start = ((), (), s32[]{:S(2)}) async-start(), calls=%async_computation.1 | async-start | bytes 3538944 | tf_op jit(solution)/shard_map/all_gather | solution.py:101
  10.5 8.8 %copy-start.16 = (f32[32,768]{1,0:T(8,128)}, f32[32,768]{1,0:T(8,128)S(1)}, u32[]{:S(2)}) copy-start(f32[32,768]{1,0:T(8,128)S(1)} %fusion.27) | copy-start | bytes 294916
  12.3 7.1 %copy-start.18 = (f32[32,768]{1,0:T(8,128)}, f32[32,768]{1,0:T(8,128)S(1)}, u32[]{:S(2)}) copy-start(f32[32,768]{1,0:T(8,128)S(1)} %fusion.97) | copy-start | bytes 294916
  12.7 6.7 %copy-start.27 = (f32[8,32]{1,0:T(8,128)}, f32[8,32]{1,0:T(8,128)S(1)}, u32[]{:S(2)}) copy-start(f32[8,32]{1,0:T(8,128)S(1)} %add_rsqrt_fusion.3) | copy-start | bytes 3076
  13.7 5.7 %copy-start.41 = (bf16[768,384]{1,0:T(8,128)(2,1)S(1)}, bf16[768,384]{1,0:T(8,128)(2,1)}, u32[]{:S(2)}) copy-start(bf16[768,384]{1,0:T(8,128)(2,1)} %param.38) | copy-start | bytes 1769476
  14.9 6.2 %copy-start.46 = (s32[32]{0:T(128)S(1)}, s32[32]{0:T(128)}, u32[]{:S(2)}) copy-start(s32[32]{0:T(128)} %param.32) | copy-start | bytes 388
  14.9 28.0 %copy-start.13 = (bf16[128,128]{1,0:T(8,128)(2,1)S(1)}, bf16[128,128]{1,0:T(8,128)(2,1)}, u32[]{:S(2)}) copy-start(bf16[128,128]{1,0:T(8,128)(2,1)} %param.43) | copy-start | bytes 98308
  14.9 29.6 %copy-start.38 = (s32[128]{0:T(128)S(1)}, s32[128]{0:T(128)}, u32[]{:S(2)}) copy-start(s32[128]{0:T(128)} %param.44) | copy-start | bytes 1540
  15.7 31.1 %copy-start.23 = (bf16[128,128]{1,0:T(8,128)(2,1)S(1)}, bf16[128,128]{1,0:T(8,128)(2,1)}, u32[]{:S(2)}) copy-start(bf16[128,128]{1,0:T(8,128)(2,1)} %param.50) | copy-start | bytes 98308
  15.7 32.0 %copy-start.12 = (bf16[4,16,32,128]{3,2,1,0:T(8,128)(2,1)S(1)}, bf16[4,16,32,128]{3,2,1,0:T(8,128)(2,1)}, u32[]{:S(2)}) copy-start(bf16[4,16,32,128]{3,2,1,0:T(8,128)(2,1)} %param.47) | copy-start | bytes 1572868
  15.7 32.0 %copy-start.32 = (bf16[16,4]{0,1:T(4,128)(2,1)S(1)}, bf16[16,4]{0,1:T(4,128)(2,1)}, u32[]{:S(2)}) copy-start(bf16[16,4]{0,1:T(4,128)(2,1)} %param.56) | copy-start | bytes 388
  15.7 5.4 %all-to-all-start = ((f32[16,32,128]{2,1,0:T(8,128)}), f32[16,32,128]{2,1,0:T(8,128)S(1)}, u32[]{:S(2)}, u32[]{:S(2)}) async-start(f32[16,32,128]{2,1,0:T(8,128)} %copy.68), calls=%async_computation | async-start | bytes 524288 | tf_op jit(solution)/shard_map/all_to_all | solution.py:82
  19.3 92.5 %all-reduce.3.cloned.1.call-start = ((), (), s32[]{:S(2)}) async-start(), calls=%async_computation.2 | async-start | bytes 786432 | tf_op jit(solution)/shard_map/psum | solution.py:127
  93.4 20.5 %copy-start.42 = (bf16[768,128]{1,0:T(8,128)(2,1)S(1)}, bf16[768,128]{1,0:T(8,128)(2,1)}, u32[]{:S(2)}) copy-start(bf16[768,128]{1,0:T(8,128)(2,1)} %param.48) | copy-start | bytes 589828
  93.4 25.5 %copy-start.31 = (s32[128]{0:T(128)S(1)}, s32[128]{0:T(128)}, u32[]{:S(2)}) copy-start(s32[128]{0:T(128)} %get-tuple-element.10) | copy-start | bytes 1540
  93.4 25.5 %copy-start.14 = (bf16[128,128]{1,0:T(8,128)(2,1)S(1)}, bf16[128,128]{1,0:T(8,128)(2,1)}, u32[]{:S(2)}) copy-start(bf16[128,128]{1,0:T(8,128)(2,1)} %param.43) | copy-start | bytes 98308
  94.1 25.0 %copy-start.22 = (f32[128,128]{1,0:T(8,128)S(1)}, f32[128,128]{1,0:T(8,128)}, u32[]{:S(2)}) copy-start(f32[128,128]{1,0:T(8,128)} %fusion.30) | copy-start | bytes 196612
  95.7 27.6 %copy-start.24 = (pred[128]{0:T(512)(128)(4,1)S(1)}, pred[128]{0:T(512)(128)(4,1)}, u32[]{:S(2)}) copy-start(pred[128]{0:T(512)(128)(4,1)} %get-tuple-element.9) | copy-start | bytes 388
  113.1 10.5 %copy-start.20 = (f32[128,128]{0,1:T(8,128)S(1)}, f32[128,128]{0,1:T(8,128)}, u32[]{:S(2)}) copy-start(f32[128,128]{0,1:T(8,128)} %fusion.96) | copy-start | bytes 196612
  113.1 10.5 %copy-start.43 = (bf16[128,128]{1,0:T(8,128)(2,1)S(1)}, bf16[128,128]{1,0:T(8,128)(2,1)}, u32[]{:S(2)}) copy-start(bf16[128,128]{1,0:T(8,128)(2,1)} %param.53) | copy-start | bytes 98308
  113.8 10.2 %copy-start.44 = (bf16[128,128]{1,0:T(8,128)(2,1)S(1)}, bf16[128,128]{1,0:T(8,128)(2,1)}, u32[]{:S(2)}) copy-start(bf16[128,128]{1,0:T(8,128)(2,1)} %param.52) | copy-start | bytes 98308
  114.2 5.0 %collective-permute-start = (bf16[8,16,128]{2,1,0:T(8,128)(2,1)S(1)}, bf16[8,16,128]{2,1,0:T(8,128)(2,1)S(1)}, u32[]{:S(2)}, u32[]{:S(2)}) collective-permute-start(bf16[8,16,128]{2,1,0:T(8,128)(2,1)S(1)} %get-tuple-element.19), channel_id=1, source_target_pairs={{0,2},{2,4},{4,6},{6,8},{8,10},{10,12},{12,14},{1,3},{3,5},{5,7},{... | collective-permute-start | bytes 98312 | tf_op jit(solution)/shard_map/ppermute | solution.py:21
  117.6 4.7 %collective-permute-start.1 = (bf16[8,16,128]{2,1,0:T(8,128)(2,1)S(1)}, bf16[8,16,128]{2,1,0:T(8,128)(2,1)S(1)}, u32[]{:S(2)}, u32[]{:S(2)}) collective-permute-start(bf16[8,16,128]{2,1,0:T(8,128)(2,1)S(1)} %get-tuple-element.20), channel_id=1, source_target_pairs={{2,0},{4,2},{6,4},{8,6},{10,8},{12,10},{14,12},{3,1},{5,3},{7,5},{... | collective-permute-start | bytes 98312 | tf_op jit(solution)/shard_map/ppermute | solution.py:23
  119.1 14.2 %copy-start.11 = (f32[128,128]{0,1:T(8,128)}, f32[128,128]{0,1:T(8,128)S(1)}, u32[]{:S(2)}) copy-start(f32[128,128]{0,1:T(8,128)S(1)} %copy.72) | copy-start | bytes 196612
  119.2 14.1 %copy-start.21 = (f32[128,128]{0,1:T(8,128)}, f32[128,128]{0,1:T(8,128)S(1)}, u32[]{:S(2)}) copy-start(f32[128,128]{0,1:T(8,128)S(1)} %copy.75) | copy-start | bytes 196612
  123.1 9.6 %copy-start.10 = (f32[4,4,32,128]{3,1,2,0:T(4,128)S(1)}, f32[4,4,32,128]{3,1,2,0:T(4,128)}, u32[]{:S(2)}) copy-start(f32[4,4,32,128]{3,1,2,0:T(4,128)} %convolution_bitcast_fusion.1) | copy-start | bytes 786436
  123.3 10.0 %copy-start.3 = (bf16[128,8,128]{0,2,1:T(8,128)(2,1)}, bf16[128,8,128]{0,2,1:T(8,128)(2,1)S(1)}, u32[]{:S(2)}) copy-start(bf16[128,8,128]{0,2,1:T(8,128)(2,1)S(1)} %copy.74) | copy-start | bytes 786436
  123.4 9.3 %copy-start.47 = (s32[128]{0:T(128)S(1)}, s32[128]{0:T(128)}, u32[]{:S(2)}) copy-start(s32[128]{0:T(128)} %param.46) | copy-start | bytes 1540
  123.5 9.9 %copy-start.45 = (bf16[128,128]{1,0:T(8,128)(2,1)S(1)}, bf16[128,128]{1,0:T(8,128)(2,1)}, u32[]{:S(2)}) copy-start(bf16[128,128]{1,0:T(8,128)(2,1)} %param.51) | copy-start | bytes 98308
  123.6 9.7 %copy-start.29 = (f32[8,128]{1,0:T(8,128)}, f32[8,128]{1,0:T(8,128)S(1)}, u32[]{:S(2)}) copy-start(f32[8,128]{1,0:T(8,128)S(1)} %add_rsqrt_fusion.1) | copy-start | bytes 12292
  125.1 9.1 %collective-permute-start.2 = (bf16[2,8,64,128]{3,2,1,0:T(8,128)(2,1)}, bf16[2,8,64,128]{3,2,1,0:T(8,128)(2,1)}, u32[]{:S(2)}, u32[]{:S(2)}) collective-permute-start(bf16[2,8,64,128]{3,2,1,0:T(8,128)(2,1)} %get-tuple-element.17), channel_id=1, source_target_pairs={{0,1},{1,2},{2,3},{3,4},{4,5},{5,6},{6,7},{7,8},{8,9},{9,10},{10,1... | collective-permute-start | bytes 786440 | tf_op jit(solution)/shard_map/ppermute | solution.py:21
  130.6 7.8 %collective-permute-start.3 = (bf16[2,8,64,128]{3,2,1,0:T(8,128)(2,1)S(1)}, bf16[2,8,64,128]{3,2,1,0:T(8,128)(2,1)}, u32[]{:S(2)}, u32[]{:S(2)}) collective-permute-start(bf16[2,8,64,128]{3,2,1,0:T(8,128)(2,1)S(1)} %get-tuple-element.18), channel_id=1, source_target_pairs={{1,0},{2,1},{3,2},{4,3},{5,4},{6,5},{7,6},{8,7},{9,8},{10,9},{11,1... | collective-permute-start | bytes 786440 | tf_op jit(solution)/shard_map/ppermute | solution.py:23
  (23 other events, 52.9 us)
Sparse Core Ops, SparseCore 0:
  14.6 62.0 all-gather.2
  93.5 18.2 all-reduce.2
where the time goes:
time: 171 us; the launch traced here: 170 us
  waiting for transfers between devices  51.6 us (30%)
  local copies, waits for them, and re-layouts  28.7 us (17%)
  matrix products  21.5 us (13%)
  blocking collectives  19.5 us (11%)
  other arithmetic  16.6 us (10%)
  starting transfers between devices  16 us (9%)
  between operations  15.7 us (9%)
    all_gather x1, waiting for transfers between devices, shards(): kv_piece = lax.all_gather(stacked, 'row', axis=2, tiled=True)  28 us
    unnamed x1, blocking collectives  19.5 us
    psum x1, waiting for transfers between devices, shards(): lax.psum(partial_value.astype(jnp.bfloat16), 'col').astype(jnp.float32)  16.1 us
    ppermute x2, starting transfers between devices, extended_2(): lax.ppermute(tail, axis, [(i, (i + 1) % count) for i in range(ends)])  8.97 us
    ppermute x2, waiting for transfers between devices, extended_2(): lax.ppermute(head, axis, [((i + 1) % count, i) for i in range(ends)])  7.27 us
    slice x2, local copies, waits for them, and re-layouts, shards(): piece_keys = kv_piece[0].reshape(samples, key_count, local_heads, HEAD)  5.09 us
    all_to_all x1, starting transfers between devices, shards(): lax.all_to_all(local_bias, 'col', split_axis=0, concat_axis=2, tiled=True)  3.62 us
  transfers between devices with their start and end apart: 7, of which 5 were waited for; matrix products, arithmetic and copies ran while one was open for 8% of the time, Pallas kernels for 0%

commit v1 on v0

v1 whole, which is shorter than its diff:
```python
import functools

import jax
import jax.numpy as jnp
from jax import lax
from jax.experimental import pallas as pl
from jax.experimental.pallas import tpu as pltpu
from jax.sharding import PartitionSpec as P

HEAD = 48
AHEADS = 4
AHEAD = 32
WQ = 32
WK = 128
CHUNKS = 2
F32 = jnp.float32
BF16 = jnp.bfloat16


def layer_norm(inputs):
    inputs = inputs.astype(F32)
    centred = inputs - jnp.mean(inputs, axis=-1, keepdims=True)
    variance = jnp.mean(centred * centred, axis=-1, keepdims=True)
    return centred * lax.rsqrt(variance + 1e-05)


def dot(a, b):
    return jnp.dot(a, b, preferred_element_type=F32)


def dot_nt(a, b):
    return lax.dot_general(a, b, (((1,), (1,)), ((), ())), preferred_element_type=F32)


def remote(src, dst, send, recv, row, col):
    return pltpu.make_async_remote_copy(
        src_ref=src,
        dst_ref=dst,
        send_sem=send,
        recv_sem=recv,
        device_id={"row": row, "col": col},
        device_id_type=pl.DeviceIdType.MESH,
    )


def token_kernel(
    rows,
    tin, cond, tmask, pc, wpt, wsc, wsh, wog, wq, wk, wv, wg, wo, wta, acond, atok,
    tout, lk_out, ac_out, tk_out,
    mx, qb, gate, og, gated, gsib, wosib, pbs, bias, bfull, mk, lk, ac, tk,
    zs, zr, ys, yr, cs, cr, ms, mr, gs, gr, xs, xr,
):
    r = lax.axis_index("row")
    c = lax.axis_index("col")
    other = 1 - c
    samples, toks, width = tin.shape
    heads = wpt.shape[0] // 2
    half = pc.shape[1]
    total = half * 2
    n = rows // 2
    i = r // 2
    y = r % 2
    hs = samples // 2
    ns = hs // CHUNKS
    inv_root = HEAD ** (-0.5)

    def wrap(v):
        return lax.rem(v + rows, rows)

    left_row, right_row = wrap(r + c - 1), wrap(r + c)

    barrier = pltpu.get_barrier_semaphore()

    def greet(row, col):
        pl.semaphore_signal(
            barrier, inc=1, device_id={"row": row, "col": col},
            device_id_type=pl.DeviceIdType.MESH,
        )

    for d in range(1, rows):
        greet(wrap(r + d), c)
    greet(r, other)
    greet(wrap(r + 2 * c - 1), other)
    pl.semaphore_wait(barrier, rows + 1)

    cond_norm = layer_norm(cond[...]).astype(BF16)
    scale = jax.nn.sigmoid(dot(cond_norm, wsc[...]))
    shift = dot(cond_norm, wsh[...])
    for s in range(samples):
        mx[r, s] = (scale * layer_norm(tin[s]) + shift).astype(BF16)

    started = []

    def go(copy):
        copy.start()
        started.append(copy)
        return copy

    def block(row, core, j):
        return mx.at[row, pl.ds(core * hs + j * ns, ns)]

    def z_row(d):
        return lax.rem(i + n + d, n) * 2 + y

    for j in range(CHUNKS):
        own = block(r, c, j)
        for d in range(1, n):
            go(remote(own, own, zs.at[j, d - 1], zr.at[j, d - 1], z_row(d), c))
        go(remote(own, own, ys.at[j, 0], yr.at[j, 0], i * 2 + 1 - y, c))

    placed = (
        lax.broadcasted_iota(jnp.int32, (toks, total), 1)
        == lax.broadcasted_iota(jnp.int32, (toks, total), 0) + r * toks
    ).astype(F32)
    valid = jnp.broadcast_to(tmask[...], (8, toks)).astype(F32)
    mk[r] = dot(valid, placed)
    mask_copies = [
        go(remote(mk.at[r], mk.at[r], ms.at[d - 1], mr.at[d - 1], wrap(r + d), c))
        for d in range(1, rows)
    ]
    tk[1] = jnp.broadcast_to(atok[...], (8, atok.shape[1])).astype(F32)
    edge = WK // 2
    atoms = acond.shape[0]
    ac[edge : edge + atoms] = acond[...]
    wide = [
        go(remote(wo, wosib, xs.at[0], xr.at[0], r, other)),
        go(remote(tk.at[1], tk.at[0], xs.at[1], xr.at[1], right_row, other)),
        go(remote(tk.at[1], tk.at[2], xs.at[2], xr.at[2], left_row, other)),
        go(remote(ac.at[pl.ds(atoms, edge)], ac.at[pl.ds(0, edge)], xs.at[3], xr.at[3], right_row, other)),
        go(remote(ac.at[pl.ds(edge, edge)], ac.at[pl.ds(atoms + edge, edge)], xs.at[4], xr.at[4], left_row, other)),
    ]

    for q in range(toks):
        part = dot_nt(wpt[...], pc[q])
        pbs[0, q * heads : (q + 1) * heads] = part[:heads]
        pbs[1, q * heads : (q + 1) * heads] = part[heads:]
    bias_copy = go(remote(pbs.at[other], bias.at[c], xs.at[5], xr.at[5], r, other))
    bias[c] = pbs[c]

    own_rows = mx[r].reshape(samples * toks, width)
    qb[...] = (dot(own_rows, wq[...]) * inv_root).astype(BF16).astype(F32).reshape(qb.shape)
    gate[...] = jax.nn.sigmoid(dot(own_rows, wg[...])).reshape(gate.shape)
    og[...] = jax.nn.sigmoid(dot(cond_norm, wog[...]))

    def forward_z(j, d):
        src = z_row(-d)
        got = block(src, c, j)
        remote(got, got, zs.at[j, d - 1], zr.at[j, d - 1], src, c).wait_recv()
        go(remote(got, got, ys.at[j, d], yr.at[j, d], i * 2 + 1 - y, c))
        go(remote(got, got, cs.at[j, d - 1], cr.at[j, d - 1], r, other))

    def forward_y(j, d):
        src = lax.rem(i + n - d, n) * 2 + 1 - y
        got = block(src, c, j)
        remote(got, got, ys.at[j, d], yr.at[j, d], i * 2 + 1 - y, c).wait_recv()
        go(remote(got, got, cs.at[j, n - 1 + d], cr.at[j, n - 1 + d], r, other))

    def arrived(j):
        for d in range(1, n):
            got = block(z_row(-d), other, j)
            remote(got, got, cs.at[j, d - 1], cr.at[j, d - 1], r, other).wait_recv()
        for d in range(n):
            got = block(lax.rem(i + n - d, n) * 2 + 1 - y, other, j)
            remote(got, got, cs.at[j, n - 1 + d], cr.at[j, n - 1 + d], r, other).wait_recv()

    columns = wq.shape[1]
    lane = lax.broadcasted_iota(jnp.int32, (heads, columns), 1)
    first = lax.broadcasted_iota(jnp.int32, (heads, columns), 0) * HEAD
    head_mask = ((lane >= first) & (lane < first + HEAD)).astype(F32)

    def attend(s, carry):
        keys_in = mx[:, s].reshape(total, width)
        keys = dot(keys_in, wk[...]).astype(BF16)
        values = dot(keys_in, wv[...]).astype(BF16)
        wide_q = (qb[s][:, None, :] * head_mask[None]).reshape(toks * heads, columns).astype(BF16)
        scores = dot_nt(wide_q, keys) + bfull[...]
        weights = jnp.exp(scores - jnp.max(scores, axis=-1, keepdims=True))
        totals = jnp.sum(weights, axis=-1, keepdims=True)
        summed = dot(weights.astype(BF16), values) / totals
        picked = summed.reshape(toks, heads, columns) * head_mask[None]
        gated[s] = (gate[s] * jnp.sum(picked, axis=1)).astype(BF16)
        return carry

    for d in range(1, n):
        forward_z(0, d)
    for d in range(n):
        forward_y(0, d)
    for d in range(1, rows):
        slot = mk.at[wrap(r - d)]
        remote(slot, slot, ms.at[d - 1], mr.at[d - 1], r, c).wait_recv()
    got_bias = bias.at[other]
    remote(pbs.at[other], got_bias, xs.at[5], xr.at[5], r, other).wait_recv()
    shift_row = (jnp.sum(mk[...], axis=0) - 1.0)[0:1] * 10000.0
    for k in range(2):
        cut = slice(k * half, (k + 1) * half)
        bfull[:, cut] = bias[k] + shift_row[:, cut]
    gated_copies = []
    for j in range(CHUNKS):
        arrived(j)
        for part in range(2):
            base = part * hs + j * ns
            if j + 1 < CHUNKS:
                for d in range(1, n):
                    if (d - 1) * 2 // max(n - 1, 1) == part:
                        forward_z(j + 1, d)
            lax.fori_loop(base, base + ns, attend, None)
            k = j * 2 + part
            piece = pl.ds(base, ns)
            gated_copies.append(
                go(remote(gated.at[piece], gsib.at[piece], gs.at[k], gr.at[k], r, other))
            )
        if j + 1 < CHUNKS:
            for d in range(n):
                forward_y(j + 1, d)

    wide[0].wait_recv()
    own_part = dot(gated[...].reshape(samples * toks, columns), wo[...])
    for copy in gated_copies:
        copy.wait_recv()
    update = own_part + dot(gsib[...].reshape(samples * toks, columns), wosib[...])
    for s in range(samples):
        tokens = (tin[s].astype(F32) + og[...] * update[s * toks : (s + 1) * toks]).astype(BF16)
        tout[s] = tokens
        proj = dot(layer_norm(tokens).astype(BF16), wta[...]).astype(BF16)
        lk[toks : 2 * toks, s * proj.shape[1] : (s + 1) * proj.shape[1]] = proj
    mine = lk.at[pl.ds(toks, toks)]
    near = [
        go(remote(mine, lk.at[pl.ds(0, toks)], xs.at[6], xr.at[6], wrap(r + 1), c)),
        go(remote(mine, lk.at[pl.ds(2 * toks, toks)], xs.at[7], xr.at[7], wrap(r - 1), c)),
    ]
    for copy in wide[1:] + near:
        copy.wait_recv()
    lk_out[...] = lk[...]
    ac_out[...] = ac[...]
    tk_out[...] = tk[...]
    for copy in started:
        copy.wait_send()


def atom_kernel(
    lk, ac, tk, start, wap, amask, apair, wasc, wash, waq, wak, wav, wag, wao, wup, out
):
    r = lax.axis_index("row")
    c = lax.axis_index("col")
    samples = out.shape[0]
    atoms = amask.shape[1]
    da = ac.shape[1]
    span = ac.shape[0]
    edge = WK // 2
    windows = atoms // WQ
    near = lk.shape[0]
    toks = near // 3
    cond = ac[...].astype(F32)
    cond_norm = layer_norm(cond).astype(BF16)
    scale = jax.nn.sigmoid(dot(cond_norm, wasc[...]))
    shift = dot(cond_norm, wash[...])
    cols = [jnp.transpose(tk[k])[:, 0:1] for k in range(3)]
    token = jnp.concatenate([cols[0][atoms - edge :], cols[1], cols[2][:edge]], axis=0)
    token = token - (r * toks - toks).astype(F32)
    pick = (token == lax.broadcasted_iota(jnp.int32, (span, near), 1).astype(F32)).astype(BF16)
    looked = dot(pick, lk[...])

    base = (r * 2 + c) * atoms - edge
    place = lax.broadcasted_iota(jnp.int32, (WK, span), 1) - lax.broadcasted_iota(
        jnp.int32, (WK, span), 0
    )
    windowed = jnp.concatenate(
        [(place == start[w] - base).astype(F32) for w in range(windows)], axis=0
    ).astype(BF16)

    biases = []
    for w in range(windows):
        per_head = [None] * AHEADS
        for ch in range(apair.shape[1]):
            plane = apair[w, ch].astype(F32)
            for h in range(AHEADS):
                term = plane * wap[ch * AHEADS + h]
                per_head[h] = term if ch == 0 else per_head[h] + term
        biases.append(jnp.concatenate(per_head, axis=0))

    lane = lax.broadcasted_iota(jnp.int32, (1, da), 1)
    masks = [((lane >= h * AHEAD) & (lane < (h + 1) * AHEAD)).astype(F32) for h in range(AHEADS)]
    w_kv = jnp.concatenate([wak[...], wav[...]], axis=1)
    w_qg = jnp.concatenate([waq[...], wag[...]], axis=1)
    root = AHEAD ** (-0.5)
    live = amask[...].astype(F32)
    for s in range(samples):
        state = cond + looked[:, s * da : (s + 1) * da]
        mixed = (scale * layer_norm(state) + shift).astype(BF16)
        kv = dot(mixed, w_kv).astype(BF16)
        own = dot(mixed[edge : edge + atoms], w_qg)
        queries = (own[:, :da] * root).astype(BF16).astype(F32)
        gate = jax.nn.sigmoid(own[:, da:])
        wkv = dot(windowed, kv).astype(BF16)
        parts = []
        for w in range(windows):
            q = queries[w * WQ : (w + 1) * WQ]
            wide_q = jnp.concatenate([q * m for m in masks], axis=0).astype(BF16)
            here = wkv[w * WK : (w + 1) * WK]
            scores = dot_nt(wide_q, here[:, :da]) + biases[w]
            weights = jnp.exp(scores - jnp.max(scores, axis=-1, keepdims=True))
            totals = jnp.sum(weights, axis=-1, keepdims=True)
            summed = dot(weights.astype(BF16), here[:, da:]) / totals
            picked = summed[:WQ] * masks[0]
            for h in range(1, AHEADS):
                picked = picked + summed[h * WQ : (h + 1) * WQ] * masks[h]
            parts.append(picked)
        gated = (gate * jnp.concatenate(parts, axis=0)).astype(BF16)
        final = state[edge : edge + atoms] + dot(gated, wao[...])
        out[s] = dot_nt(wup[...], layer_norm(final).astype(BF16)) * live


def shards(
    rows,
    tokens_in, cond_single, token_mask, pair_cond, w_pair, w_scale, w_shift, w_outgate,
    w_query, w_key, w_value, w_gate, w_out, atom_cond, atom_token, window_start, atom_mask,
    atom_pair, w_token_atom, w_ascale, w_ashift, w_aquery, w_akey, w_avalue, w_agate, w_aout,
    w_apair, w_update,
):
    samples, toks, width = tokens_in.shape
    half = pair_cond.shape[1]
    total = 2 * half
    heads = w_pair.shape[1] // 2
    columns = w_query.shape[1]
    atoms, da = atom_cond.shape
    n = rows // 2
    vmem = pl.BlockSpec(memory_space=pltpu.VMEM)
    smem = pl.BlockSpec(memory_space=pltpu.SMEM)
    dma = pltpu.SemaphoreType.DMA
    flat = samples * toks
    flops = 2 * samples * total * width * columns * 4
    tokens_out, lookup, atoms_near, tokens_near = pl.pallas_call(
        functools.partial(token_kernel, rows),
        name="token_step",
        out_shape=(
            jax.ShapeDtypeStruct((samples, toks, width), BF16),
            jax.ShapeDtypeStruct((3 * toks, samples * da), BF16),
            jax.ShapeDtypeStruct((atoms + WK, da), BF16),
            jax.ShapeDtypeStruct((3, 8, atoms), F32),
        ),
        in_specs=[vmem] * 16,
        out_specs=[vmem] * 4,
        scratch_shapes=[
            pltpu.VMEM((rows, samples, toks, width), BF16),
            pltpu.VMEM((samples, toks, columns), F32),
            pltpu.VMEM((samples, toks, columns), F32),
            pltpu.VMEM((toks, width), F32),
            pltpu.VMEM((samples, toks, columns), BF16),
            pltpu.VMEM((samples, toks, columns), BF16),
            pltpu.VMEM((columns, width), BF16),
            pltpu.VMEM((2, toks * heads, half), F32),
            pltpu.VMEM((2, toks * heads, half), F32),
            pltpu.VMEM((toks * heads, total), F32),
            pltpu.VMEM((rows, 8, total), F32),
            pltpu.VMEM((3 * toks, samples * da), BF16),
            pltpu.VMEM((atoms + WK, da), BF16),
            pltpu.VMEM((3, 8, atoms), F32),
            dma((CHUNKS, n - 1)),
            dma((CHUNKS, n - 1)),
            dma((CHUNKS, n)),
            dma((CHUNKS, n)),
            dma((CHUNKS, rows - 1)),
            dma((CHUNKS, rows - 1)),
            dma((rows - 1,)),
            dma((rows - 1,)),
            dma((2 * CHUNKS,)),
            dma((2 * CHUNKS,)),
            dma((8,)),
            dma((8,)),
        ],
        compiler_params=pltpu.CompilerParams(
            collective_id=0, has_side_effects=True, vmem_limit_bytes=56 * 2**20
        ),
        cost_estimate=pl.CostEstimate(
            flops=flops, bytes_accessed=12 * 2**20, transcendentals=flat * total * heads
        ),
    )(
        tokens_in, cond_single, token_mask.reshape(1, toks), pair_cond, w_pair.T, w_scale, w_shift,
        w_outgate, w_query, w_key, w_value, w_gate, w_out, w_token_atom, atom_cond,
        atom_token.reshape(1, atoms),
    )
    atom_update = pl.pallas_call(
        atom_kernel,
        name="atom_step",
        out_shape=jax.ShapeDtypeStruct((samples, 3, atoms), F32),
        in_specs=[vmem] * 3 + [smem] * 2 + [vmem] * 10,
        out_specs=vmem,
        compiler_params=pltpu.CompilerParams(vmem_limit_bytes=32 * 2**20),
        cost_estimate=pl.CostEstimate(
            flops=2 * samples * atoms * da * 3000, bytes_accessed=2**20, transcendentals=2**19
        ),
    )(
        lookup, atoms_near, tokens_near, window_start, w_apair.astype(F32).reshape(-1),
        atom_mask.reshape(1, atoms), atom_pair, w_ascale, w_ashift, w_aquery, w_akey, w_avalue,
        w_agate, w_aout, w_update,
    )
    return (tokens_out, atom_update)


def solution(mesh):
    return jax.shard_map(
        functools.partial(shards, mesh.shape["row"]),
        mesh=mesh,
        in_specs=(
            P("groups", "row", None),
            P(("groups", "row"), None),
            P(("groups", "row")),
            P(("groups", "row"), "col", None),
            P(),
            P(),
            P(),
            P(),
            P(None, "col"),
            P(None, "col"),
            P(None, "col"),
            P(None, "col"),
            P("col", None),
            P(("groups", "row", "col"), None),
            P(("groups", "row", "col")),
            P(("groups", "row", "col")),
            P(("groups", "row", "col")),
            P(("groups", "row", "col"), None, None, None),
            P(),
            P(),
            P(),
            P(),
            P(),
            P(),
            P(),
            P(),
            P(),
            P(),
        ),
        out_specs=(P("groups", "row", None), P("groups", None, ("row", "col"))),
        check_vma=False,
    )
```

time: 171 us -> 70 us (0.41)
  the two profiles are of different devices: /device:TPU:1 before, /device:TPU:0 now
where the time goes in v1:
time: 70 us; the launch traced here: 69.8 us
  Pallas kernels  64.9 us (93%)
  local copies, waits for them, and re-layouts  4.06 us (6%)
  between operations  0.85 us (1%)
    pallas_call x1, Pallas kernels, shards(): pl.pallas_call(functools.partial(token_kernel, rows), name='token_step',...  52.7 us
    pallas_call x1, Pallas kernels, shards(): pl.pallas_call(atom_kernel, name='atom_step', out_shape=jax.ShapeDtypeStr...  12.2 us
    unnamed x34, local copies, waits for them, and re-layouts  3.88 us

profile of v1, /device:TPU:0, one launch (start us, length us, event | category | flops | bytes accessed | tf_op | source)
XLA Modules:
  0.0 69.8 jit_solution(7292891241567403520)
XLA Ops:
  0.6 0.0 copy-start.15
  0.6 0.0 copy-start
  0.7 0.0 copy-start.1
  0.7 0.0 copy-start.2
  0.7 0.0 copy-start.3
  0.7 0.0 copy-start.4
  0.7 0.0 copy-start.5
  0.7 0.0 copy-start.6
  0.7 0.0 copy-start.7
  0.7 0.0 copy-start.8
  0.7 0.0 copy-start.9
  0.7 0.0 copy-start.10
  0.8 52.7 %token_step.1 = (bf16[8,32,768]{2,1,0:T(8,128)(2,1)}, bf16[96,1024]{1,0:T(8,128)(2,1)}, bf16[256,128]{1,0:T(8,128)(2,1)}, f32[3,8,128]{2,1,0:T(8,128)}) custom-call(bf16[8,32,768]{2,1,0:T(8,128)(2,1)} %tin.1, bf16[32,768]{1,0:T(8,128)(2,1)} %cond.1, s32[1,32]{1,0:T(1,128)} %bitcast.6, bf16[32,128,128]{2,1,0:T(8,128)(2,1)} %pc.1, bf16[16,128]{1,0:T(8,128)(2,1)} %bitcast.5, ...), custom_call_target="tpu_custom_call" | custom-call | flops 4831838208 | bytes 12582912 | tf_op jit(solution)/shard_map/token_step/pallas_call | solution.py:332
  53.5 0.0 copy-done.15
  53.5 0.1 copy.32
  53.6 0.1 reshape.24.wap
  53.7 0.0 copy-done
  53.7 0.0 copy-done.1
  53.7 0.0 copy-done.2
  53.7 0.0 copy-done.3
  53.7 0.0 copy-done.4
  53.7 0.0 copy-done.5
  53.8 0.0 copy-done.6
  53.8 0.0 copy-done.7
  53.8 0.0 copy-done.8
  53.8 0.0 copy-done.9
  53.8 0.9 %copy-done.11 = bf16[96,1024]{1,0:T(8,128)(2,1)S(1)} copy-done((bf16[96,1024]{1,0:T(8,128)(2,1)S(1)}, bf16[96,1024]{1,0:T(8,128)(2,1)}, u32[]{:S(2)}) %copy-start.11) | copy-done | bytes 196632
  54.7 0.8 %copy-done.12 = bf16[256,128]{1,0:T(8,128)(2,1)S(1)} copy-done((bf16[256,128]{1,0:T(8,128)(2,1)S(1)}, bf16[256,128]{1,0:T(8,128)(2,1)}, u32[]{:S(2)}) %copy-start.12) | copy-done | bytes 65560
  55.6 0.7 %copy-done.13 = f32[3,8,128]{2,1,0:T(8,128)S(1)} copy-done((f32[3,8,128]{2,1,0:T(8,128)S(1)}, f32[3,8,128]{2,1,0:T(8,128)}, u32[]{:S(2)}) %copy-start.13) | copy-done | bytes 12312
  56.3 12.2 %atom_step.1 = f32[8,3,128]{2,1,0:T(4,128)S(1)} custom-call(bf16[96,1024]{1,0:T(8,128)(2,1)S(1)} %copy-done.11, bf16[256,128]{1,0:T(8,128)(2,1)S(1)} %copy-done.12, f32[3,8,128]{2,1,0:T(8,128)S(1)} %copy-done.13, s32[4]{0:T(128)S(1)} %copy-done.9, f32[64]{0:T(128)S(1)} %reshape.24.wap, s32[1,128]{1,0:T(1,128)S(1)} %bitcast.4, ...), custom_call_target="tpu_custom_call" | custom-call | flops 786432000 | bytes 1048576 | tf_op jit(solution)/shard_map/atom_step/pallas_call | solution.py:382
  68.4 0.6 copy.33
  69.0 0.7 %copy.35 = bf16[8,32,768]{2,1,0:T(8,128)(2,1)} copy(bf16[8,32,768]{2,1,0:T(8,128)(2,1)S(1)} %copy-done.14) | data formatting | bytes 786432
  (6 shorter events, 0.0 us)
Async XLA Ops:
  0.6 52.9 %copy-start.15 = (bf16[16,4]{0,1:T(4,128)(2,1)S(1)}, bf16[16,4]{0,1:T(4,128)(2,1)}, u32[]{:S(2)}) copy-start(bf16[16,4]{0,1:T(4,128)(2,1)} %param.54) | copy-start | bytes 388
  0.6 53.0 %copy-start = (bf16[4,16,32,128]{3,2,1,0:T(8,128)(2,1)S(1)}, bf16[4,16,32,128]{3,2,1,0:T(8,128)(2,1)}, u32[]{:S(2)}) copy-start(bf16[4,16,32,128]{3,2,1,0:T(8,128)(2,1)} %apair.1) | copy-start | bytes 1572868
  0.7 53.0 %copy-start.1 = (bf16[128,128]{1,0:T(8,128)(2,1)S(1)}, bf16[128,128]{1,0:T(8,128)(2,1)}, u32[]{:S(2)}) copy-start(bf16[128,128]{1,0:T(8,128)(2,1)} %wasc.1) | copy-start | bytes 98308
  0.7 53.0 %copy-start.2 = (bf16[128,128]{1,0:T(8,128)(2,1)S(1)}, bf16[128,128]{1,0:T(8,128)(2,1)}, u32[]{:S(2)}) copy-start(bf16[128,128]{1,0:T(8,128)(2,1)} %wash.1) | copy-start | bytes 98308
  0.7 53.0 %copy-start.3 = (bf16[128,128]{1,0:T(8,128)(2,1)S(1)}, bf16[128,128]{1,0:T(8,128)(2,1)}, u32[]{:S(2)}) copy-start(bf16[128,128]{1,0:T(8,128)(2,1)} %waq.1) | copy-start | bytes 98308
  0.7 53.0 %copy-start.4 = (bf16[128,128]{1,0:T(8,128)(2,1)S(1)}, bf16[128,128]{1,0:T(8,128)(2,1)}, u32[]{:S(2)}) copy-start(bf16[128,128]{1,0:T(8,128)(2,1)} %wak.1) | copy-start | bytes 98308
  0.7 53.0 %copy-start.5 = (bf16[128,128]{1,0:T(8,128)(2,1)S(1)}, bf16[128,128]{1,0:T(8,128)(2,1)}, u32[]{:S(2)}) copy-start(bf16[128,128]{1,0:T(8,128)(2,1)} %wav.1) | copy-start | bytes 98308
  0.7 53.0 %copy-start.6 = (bf16[128,128]{1,0:T(8,128)(2,1)S(1)}, bf16[128,128]{1,0:T(8,128)(2,1)}, u32[]{:S(2)}) copy-start(bf16[128,128]{1,0:T(8,128)(2,1)} %wag.1) | copy-start | bytes 98308
  0.7 53.0 %copy-start.7 = (bf16[128,128]{1,0:T(8,128)(2,1)S(1)}, bf16[128,128]{1,0:T(8,128)(2,1)}, u32[]{:S(2)}) copy-start(bf16[128,128]{1,0:T(8,128)(2,1)} %wao.1) | copy-start | bytes 98308
  0.7 53.0 %copy-start.8 = (bf16[3,128]{1,0:T(4,128)(2,1)S(1)}, bf16[3,128]{1,0:T(4,128)(2,1)}, u32[]{:S(2)}) copy-start(bf16[3,128]{1,0:T(4,128)(2,1)} %wup.1) | copy-start | bytes 2308
  0.7 53.0 %copy-start.9 = (s32[4]{0:T(128)S(1)}, s32[4]{0:T(128)}, u32[]{:S(2)}) copy-start(s32[4]{0:T(128)} %start.1) | copy-start | bytes 52
  0.7 53.0 %copy-start.10 = (s32[128]{0:T(128)S(1)}, s32[128]{0:T(128)}, u32[]{:S(2)}) copy-start(s32[128]{0:T(128)} %param.44) | copy-start | bytes 1540
  53.8 0.9 %copy-start.11 = (bf16[96,1024]{1,0:T(8,128)(2,1)S(1)}, bf16[96,1024]{1,0:T(8,128)(2,1)}, u32[]{:S(2)}) copy-start(bf16[96,1024]{1,0:T(8,128)(2,1)} %get-tuple-element.7.lk) | copy-start | bytes 589828
  54.7 0.8 %copy-start.12 = (bf16[256,128]{1,0:T(8,128)(2,1)S(1)}, bf16[256,128]{1,0:T(8,128)(2,1)}, u32[]{:S(2)}) copy-start(bf16[256,128]{1,0:T(8,128)(2,1)} %get-tuple-element.8.ac) | copy-start | bytes 196612
  55.6 0.7 %copy-start.13 = (f32[3,8,128]{2,1,0:T(8,128)S(1)}, f32[3,8,128]{2,1,0:T(8,128)}, u32[]{:S(2)}) copy-start(f32[3,8,128]{2,1,0:T(8,128)} %get-tuple-element.9.tk) | copy-start | bytes 36868
  56.3 12.8 %copy-start.14 = (bf16[8,32,768]{2,1,0:T(8,128)(2,1)S(1)}, bf16[8,32,768]{2,1,0:T(8,128)(2,1)}, u32[]{:S(2)}) copy-start(bf16[8,32,768]{2,1,0:T(8,128)(2,1)} %get-tuple-element.16) | copy-start | bytes 1179652

commit v2 on v1

v2 whole, which is shorter than its diff:
```python
import functools

import jax
import jax.numpy as jnp
from jax import lax
from jax.experimental import pallas as pl
from jax.experimental.pallas import tpu as pltpu
from jax.sharding import PartitionSpec as P

HEAD = 48
AHEADS = 4
AHEAD = 32
WQ = 32
WK = 128
CHUNKS = 2
F32 = jnp.float32
BF16 = jnp.bfloat16


def layer_norm(inputs):
    inputs = inputs.astype(F32)
    centred = inputs - jnp.mean(inputs, axis=-1, keepdims=True)
    variance = jnp.mean(centred * centred, axis=-1, keepdims=True)
    return centred * lax.rsqrt(variance + 1e-05)


def dot(a, b):
    return jnp.dot(a, b, preferred_element_type=F32)


def dot_nt(a, b):
    return lax.dot_general(a, b, (((1,), (1,)), ((), ())), preferred_element_type=F32)


def remote(src, dst, send, recv, row, col):
    return pltpu.make_async_remote_copy(
        src_ref=src,
        dst_ref=dst,
        send_sem=send,
        recv_sem=recv,
        device_id={"row": row, "col": col},
        device_id_type=pl.DeviceIdType.MESH,
    )


def step_kernel(
    rows,
    cond, tmask, wpt, acond, atok, amask, start, wap, wasc, wash, waq, wak, wav, wag, wao, wup,
    tin_h, wsc_h, wsh_h, pc_h, wq_h, wg_h, wo_h, wog_h, wk_h, wv_h, wta_h, apair_h,
    tout, out,
    tin, wsc, wsh, pc, wq, wg, wo, wog, wk, wv, wta, apair,
    mx, qb, gate, og, gated, gsib, wosib, pbs, bias, bfull, mk, lk, ac, tk,
    asc, ash, pick, windowed, abias,
    ls, zs, zr, ys, yr, cs, cr, ms, mr, gs, gr, xs, xr,
):
    r = lax.axis_index("row")
    c = lax.axis_index("col")
    other = 1 - c
    samples, toks, width = tin.shape
    heads = wpt.shape[0] // 2
    half = pc.shape[1]
    total = half * 2
    n = rows // 2
    i = r // 2
    y = r % 2
    hs = samples // 2
    ns = hs // CHUNKS
    inv_root = HEAD ** (-0.5)

    def wrap(v):
        return lax.rem(v + rows, rows)

    left_row, right_row = wrap(r + c - 1), wrap(r + c)

    pairs = [
        (tin_h, tin), (wsc_h, wsc), (wsh_h, wsh), (pc_h, pc), (wq_h, wq), (wg_h, wg), (wo_h, wo),
        (wog_h, wog), (wk_h, wk), (wv_h, wv), (wta_h, wta), (apair_h, apair),
    ]
    loads = [pltpu.make_async_copy(src, dst, ls.at[k]) for k, (src, dst) in enumerate(pairs)]
    for load in loads[:3]:
        load.start()

    barrier = pltpu.get_barrier_semaphore()

    def greet(row, col):
        pl.semaphore_signal(
            barrier, inc=1, device_id={"row": row, "col": col},
            device_id_type=pl.DeviceIdType.MESH,
        )

    for d in range(1, rows):
        greet(wrap(r + d), c)
    greet(r, other)
    greet(wrap(r + 2 * c - 1), other)

    cond_norm = layer_norm(cond[...]).astype(BF16)
    for load in loads[:3]:
        load.wait()
    for load in loads[3:]:
        load.start()
    scale = jax.nn.sigmoid(dot(cond_norm, wsc[...]))
    shift = dot(cond_norm, wsh[...])
    for s in range(samples):
        mx[r, s] = (scale * layer_norm(tin[s]) + shift).astype(BF16)
    pl.semaphore_wait(barrier, rows + 1)

    started = []

    def go(copy):
        copy.start()
        started.append(copy)
        return copy

    def block(row, core, j):
        return mx.at[row, pl.ds(core * hs + j * ns, ns)]

    steps = [(t, way) for t in range(1, n) for way in (0, 1)]
    ids = {step: k for k, step in enumerate(steps)}
    partner = i * 2 + 1 - y

    def valid(step):
        t, way = step
        return i >= t if way == 0 else i + t < n

    def line(step):
        t, way = step
        return lax.rem(i + n - t, n) if way == 0 else lax.rem(i + t, n)

    def z_copy(j, step):
        t, way = step
        back = t - 1
        src = lax.rem(i + n - back, n) if way == 0 else lax.rem(i + back, n)
        dest = lax.rem(i + 1, n) if way == 0 else lax.rem(i + n - 1, n)
        ref = block(src * 2 + y, c, j)
        k = ids[step]
        return remote(ref, ref, zs.at[j, k], zr.at[j, k], dest * 2 + y, c)

    def z_sends(step):
        t, way = step
        if way == 0:
            return (i + 1 < n) & (i + 1 >= t)
        return (i >= 1) & (i + t <= n)

    def y_copy(j, k):
        src = i if k == 0 else line(steps[k - 1])
        ref = block(src * 2 + y, c, j)
        return remote(ref, ref, ys.at[j, k], yr.at[j, k], partner, c)

    def c_copy(j, k, over_y, core):
        src = i if k == 0 else line(steps[k - 1])
        col = 1 - y if over_y else y
        ref = block(src * 2 + col, core, j)
        slot = len(steps) + k if over_y else k - 1
        return remote(ref, ref, cs.at[j, slot], cr.at[j, slot], r, other)

    def y_arriving(j, k):
        src = i if k == 0 else line(steps[k - 1])
        ref = block(src * 2 + 1 - y, c, j)
        return remote(ref, ref, ys.at[j, k], yr.at[j, k], partner, c)

    def z_arriving(j, step):
        ref = block(line(step) * 2 + y, c, j)
        k = ids[step]
        return remote(ref, ref, zs.at[j, k], zr.at[j, k], r, other)

    def send_own(j):
        for way in (0, 1):
            pl.when(z_sends((1, way)))(lambda: z_copy(j, (1, way)).start())
        y_copy(j, 0).start()

    def forward_z(j, t):
        for way in (0, 1):
            step = (t, way)

            @pl.when(valid(step))
            def _():
                z_arriving(j, step).wait_recv()
                if t + 1 < n:
                    pl.when(z_sends((t + 1, way)))(lambda: z_copy(j, (t + 1, way)).start())
                y_copy(j, ids[step] + 1).start()
                c_copy(j, ids[step] + 1, False, c).start()

    def forward_y(j, t):
        if t == 0:
            y_arriving(j, 0).wait_recv()
            c_copy(j, 0, True, c).start()
            return
        for way in (0, 1):
            step = (t, way)

            @pl.when(valid(step))
            def _():
                y_arriving(j, ids[step] + 1).wait_recv()
                c_copy(j, ids[step] + 1, True, c).start()

    def arrived(j):
        c_copy(j, 0, True, other).wait_recv()
        for step in steps:

            @pl.when(valid(step))
            def _():
                c_copy(j, ids[step] + 1, False, other).wait_recv()
                c_copy(j, ids[step] + 1, True, other).wait_recv()

    def all_sent(j):
        y_copy(j, 0).wait_send()
        c_copy(j, 0, True, c).wait_send()
        for step in steps:
            pl.when(z_sends(step))(lambda: z_copy(j, step).wait_send())

            @pl.when(valid(step))
            def _():
                y_copy(j, ids[step] + 1).wait_send()
                c_copy(j, ids[step] + 1, False, c).wait_send()
                c_copy(j, ids[step] + 1, True, c).wait_send()

    send_own(0)

    placed = (
        lax.broadcasted_iota(jnp.int32, (toks, total), 1)
        == lax.broadcasted_iota(jnp.int32, (toks, total), 0) + r * toks
    ).astype(F32)
    present = jnp.broadcast_to(tmask[...], (8, toks)).astype(F32)
    mk[r] = dot(present, placed)
    for d in range(1, rows):
        go(remote(mk.at[r], mk.at[r], ms.at[d - 1], mr.at[d - 1], wrap(r + d), c))
    tk[1] = jnp.broadcast_to(atok[...], (8, atok.shape[1])).astype(F32)
    edge = WK // 2
    atoms = acond.shape[0]
    ac[edge : edge + atoms] = acond[...]
    edges = [
        go(remote(tk.at[1], tk.at[0], xs.at[1], xr.at[1], right_row, other)),
        go(remote(tk.at[1], tk.at[2], xs.at[2], xr.at[2], left_row, other)),
        go(remote(ac.at[pl.ds(atoms, edge)], ac.at[pl.ds(0, edge)], xs.at[3], xr.at[3], right_row, other)),
        go(remote(ac.at[pl.ds(edge, edge)], ac.at[pl.ds(atoms + edge, edge)], xs.at[4], xr.at[4], left_row, other)),
    ]

    loads[3].wait()
    for q in range(toks):
        part = dot_nt(wpt[...], pc[q])
        pbs[0, q * heads : (q + 1) * heads] = part[:heads]
        pbs[1, q * heads : (q + 1) * heads] = part[heads:]
    bias_copy = go(remote(pbs.at[other], bias.at[c], xs.at[5], xr.at[5], r, other))
    bias[c] = pbs[c]
    forward_z(0, 1)
    forward_y(0, 0)
    send_own(1)

    for load in loads[4:7]:
        load.wait()
    wide_out = go(remote(wo, wosib, xs.at[0], xr.at[0], r, other))
    own_rows = mx[r].reshape(samples * toks, width)
    qb[...] = (dot(own_rows, wq[...]) * inv_root).astype(BF16).astype(F32).reshape(qb.shape)
    gate[...] = jax.nn.sigmoid(dot(own_rows, wg[...])).reshape(gate.shape)
    forward_z(0, 2)
    forward_y(0, 1)
    loads[7].wait()
    og[...] = jax.nn.sigmoid(dot(cond_norm, wog[...]))

    for copy in edges:
        copy.wait_recv()
    da = ac.shape[1]
    span = ac.shape[0]
    windows = atoms // WQ
    near = lk.shape[0]
    atom_cond = ac[...].astype(F32)
    atom_norm = layer_norm(atom_cond).astype(BF16)
    asc[...] = jax.nn.sigmoid(dot(atom_norm, wasc[...]))
    ash[...] = dot(atom_norm, wash[...])
    cols = [jnp.transpose(tk[k])[:, 0:1] for k in range(3)]
    token = jnp.concatenate([cols[0][atoms - edge :], cols[1], cols[2][:edge]], axis=0)
    token = token - (r * toks - toks).astype(F32)
    pick[...] = (
        token == lax.broadcasted_iota(jnp.int32, (span, near), 1).astype(F32)
    ).astype(BF16)
    base = (r * 2 + c) * atoms - edge
    place = lax.broadcasted_iota(jnp.int32, (WK, span), 1) - lax.broadcasted_iota(
        jnp.int32, (WK, span), 0
    )
    for w in range(windows):
        windowed[w * WK : (w + 1) * WK] = (place == start[w] - base).astype(F32).astype(BF16)
    for t in range(3, n):
        forward_z(0, t)
    loads[11].wait()
    for h in range(AHEADS):
        acc = apair[:, 0].astype(F32) * wap[h]
        for ch in range(1, apair.shape[1]):
            acc = acc + apair[:, ch].astype(F32) * wap[ch * AHEADS + h]
        abias[:, h * WQ : (h + 1) * WQ] = acc
    for t in range(2, n):
        forward_y(0, t)

    columns = wq.shape[1]
    lane = lax.broadcasted_iota(jnp.int32, (heads, columns), 1)
    first = lax.broadcasted_iota(jnp.int32, (heads, columns), 0) * HEAD
    head_mask = ((lane >= first) & (lane < first + HEAD)).astype(F32)

    def attend(s, carry):
        keys_in = mx[:, s].reshape(total, width)
        keys = dot(keys_in, wk[...]).astype(BF16)
        values = dot(keys_in, wv[...]).astype(BF16)
        values = jnp.concatenate([values, jnp.ones((total, 128), BF16)], axis=1)
        wide_q = (qb[s][:, None, :] * head_mask[None]).reshape(toks * heads, columns).astype(BF16)
        scores = dot_nt(wide_q, keys) + bfull[...]
        weights = jnp.exp(scores - jnp.max(scores, axis=-1, keepdims=True))
        summed = dot(weights.astype(BF16), values)
        inverse = 1.0 / summed[:, columns:]
        summed = summed[:, :columns] * jnp.concatenate([inverse] * (columns // 128), axis=1)
        picked = summed.reshape(toks, heads, columns) * head_mask[None]
        gated[s] = (gate[s] * jnp.sum(picked, axis=1)).astype(BF16)
        return carry

    for d in range(1, rows):
        slot = mk.at[wrap(r - d)]
        remote(slot, slot, ms.at[d - 1], mr.at[d - 1], r, other).wait_recv()
    bias_copy.wait_recv()
    shift_row = (jnp.sum(mk[...], axis=0) - 1.0)[0:1] * 10000.0
    for k in range(2):
        cut = slice(k * half, (k + 1) * half)
        bfull[:, cut] = bias[k] + shift_row[:, cut]
    loads[8].wait()
    loads[9].wait()
    gated_copies = []

    def send_gated(j, part):
        piece = pl.ds(part * hs + j * ns, ns)
        k = j * 2 + part
        gated_copies.append(
            go(remote(gated.at[piece], gsib.at[piece], gs.at[k], gr.at[k], r, other))
        )

    forward_z(1, 1)
    forward_y(1, 0)
    arrived(0)
    lax.fori_loop(0, ns, attend, None)
    send_gated(0, 0)
    forward_z(1, 2)
    forward_y(1, 1)
    lax.fori_loop(hs, hs + ns, attend, None)
    send_gated(0, 1)
    for t in range(3, n):
        forward_z(1, t)
    for t in range(2, n):
        forward_y(1, t)
    arrived(1)
    lax.fori_loop(ns, 2 * ns, attend, None)
    send_gated(1, 0)
    lax.fori_loop(hs + ns, hs + 2 * ns, attend, None)
    send_gated(1, 1)

    wide_out.wait_recv()
    own_part = dot(gated[...].reshape(samples * toks, columns), wo[...])
    loads[10].wait()
    for copy in gated_copies:
        copy.wait_recv()
    update = own_part + dot(gsib[...].reshape(samples * toks, columns), wosib[...])
    for s in range(samples):
        tokens = (tin[s].astype(F32) + og[...] * update[s * toks : (s + 1) * toks]).astype(BF16)
        tout[s] = tokens
        proj = dot(layer_norm(tokens).astype(BF16), wta[...]).astype(BF16)
        lk[toks : 2 * toks, s * da : (s + 1) * da] = proj
    mine = lk.at[pl.ds(toks, toks)]
    around = [
        go(remote(mine, lk.at[pl.ds(0, toks)], xs.at[6], xr.at[6], wrap(r + 1), c)),
        go(remote(mine, lk.at[pl.ds(2 * toks, toks)], xs.at[7], xr.at[7], wrap(r - 1), c)),
    ]
    for j in range(CHUNKS):
        all_sent(j)
    for copy in started[:-2]:
        copy.wait_send()
    for copy in around:
        copy.wait_recv()

    looked = dot(pick[...], lk[...])
    lane = lax.broadcasted_iota(jnp.int32, (1, da), 1)
    masks = [((lane >= h * AHEAD) & (lane < (h + 1) * AHEAD)).astype(F32) for h in range(AHEADS)]
    w_kv = jnp.concatenate([wak[...], wav[...]], axis=1)
    w_qg = jnp.concatenate([waq[...], wag[...]], axis=1)
    root = AHEAD ** (-0.5)
    live = amask[...].astype(F32)
    ones = jnp.ones((WK, da), BF16)
    all_bias = abias[...].reshape(windows * AHEADS * WQ, WK)
    tall = AHEADS * WQ
    for s in range(samples):
        state = atom_cond + looked[:, s * da : (s + 1) * da]
        mixed = (asc[...] * layer_norm(state) + ash[...]).astype(BF16)
        kv = dot(mixed, w_kv).astype(BF16)
        own = dot(mixed[edge : edge + atoms], w_qg)
        queries = (own[:, :da] * root).astype(BF16).astype(F32)
        head_gate = jax.nn.sigmoid(own[:, da:])
        wkv = dot(windowed[...], kv).astype(BF16)
        scores = []
        for w in range(windows):
            q = queries[w * WQ : (w + 1) * WQ]
            wide_q = jnp.concatenate([q * m for m in masks], axis=0).astype(BF16)
            scores.append(dot_nt(wide_q, wkv[w * WK : (w + 1) * WK, :da]))
        scores = jnp.concatenate(scores, axis=0) + all_bias
        weights = jnp.exp(scores - jnp.max(scores, axis=-1, keepdims=True)).astype(BF16)
        parts = []
        for w in range(windows):
            wide_v = jnp.concatenate([wkv[w * WK : (w + 1) * WK, da:], ones], axis=1)
            summed = dot(weights[w * tall : (w + 1) * tall], wide_v)
            summed = summed[:, :da] / summed[:, da:]
            picked = summed[:WQ] * masks[0]
            for h in range(1, AHEADS):
                picked = picked + summed[h * WQ : (h + 1) * WQ] * masks[h]
            parts.append(picked)
        atom_gated = (head_gate * jnp.concatenate(parts, axis=0)).astype(BF16)
        final = state[edge : edge + atoms] + dot(atom_gated, wao[...])
        out[s] = dot_nt(wup[...], layer_norm(final).astype(BF16)) * live
    for copy in started[-2:]:
        copy.wait_send()


def shards(
    rows,
    tokens_in, cond_single, token_mask, pair_cond, w_pair, w_scale, w_shift, w_outgate,
    w_query, w_key, w_value, w_gate, w_out, atom_cond, atom_token, window_start, atom_mask,
    atom_pair, w_token_atom, w_ascale, w_ashift, w_aquery, w_akey, w_avalue, w_agate, w_aout,
    w_apair, w_update,
):
    samples, toks, width = tokens_in.shape
    half = pair_cond.shape[1]
    total = 2 * half
    heads = w_pair.shape[1] // 2
    columns = w_query.shape[1]
    atoms, da = atom_cond.shape
    n = rows // 2
    hops = 2 * (n - 1)
    windows = atoms // WQ
    vmem = pl.BlockSpec(memory_space=pltpu.VMEM)
    smem = pl.BlockSpec(memory_space=pltpu.SMEM)
    anywhere = pl.BlockSpec(memory_space=pl.ANY)
    dma = pltpu.SemaphoreType.DMA
    flops = 2 * samples * total * width * columns * 4
    large = (
        tokens_in, w_scale, w_shift, pair_cond, w_query, w_gate, w_out, w_outgate, w_key, w_value,
        w_token_atom, atom_pair,
    )
    tokens_out, atom_update = pl.pallas_call(
        functools.partial(step_kernel, rows),
        name="sampler_step",
        out_shape=(
            jax.ShapeDtypeStruct((samples, toks, width), BF16),
            jax.ShapeDtypeStruct((samples, 3, atoms), F32),
        ),
        in_specs=[vmem] * 6 + [smem] * 2 + [vmem] * 8 + [anywhere] * len(large),
        out_specs=[vmem] * 2,
        scratch_shapes=[pltpu.VMEM(a.shape, a.dtype) for a in large]
        + [
            pltpu.VMEM((rows, samples, toks, width), BF16),
            pltpu.VMEM((samples, toks, columns), F32),
            pltpu.VMEM((samples, toks, columns), F32),
            pltpu.VMEM((toks, width), F32),
            pltpu.VMEM((samples, toks, columns), BF16),
            pltpu.VMEM((samples, toks, columns), BF16),
            pltpu.VMEM((columns, width), BF16),
            pltpu.VMEM((2, toks * heads, half), F32),
            pltpu.VMEM((2, toks * heads, half), F32),
            pltpu.VMEM((toks * heads, total), F32),
            pltpu.VMEM((rows, 8, total), F32),
            pltpu.VMEM((3 * toks, samples * da), BF16),
            pltpu.VMEM((atoms + WK, da), BF16),
            pltpu.VMEM((3, 8, atoms), F32),
            pltpu.VMEM((atoms + WK, da), F32),
            pltpu.VMEM((atoms + WK, da), F32),
            pltpu.VMEM((atoms + WK, 3 * toks), BF16),
            pltpu.VMEM((windows * WK, atoms + WK), BF16),
            pltpu.VMEM((windows, AHEADS * WQ, WK), F32),
            dma((len(large),)),
            dma((CHUNKS, hops)),
            dma((CHUNKS, hops)),
            dma((CHUNKS, hops + 1)),
            dma((CHUNKS, hops + 1)),
            dma((CHUNKS, 2 * hops + 1)),
            dma((CHUNKS, 2 * hops + 1)),
            dma((rows - 1,)),
            dma((rows - 1,)),
            dma((2 * CHUNKS,)),
            dma((2 * CHUNKS,)),
            dma((8,)),
            dma((8,)),
        ],
        compiler_params=pltpu.CompilerParams(
            collective_id=0, has_side_effects=True, vmem_limit_bytes=56 * 2**20
        ),
        cost_estimate=pl.CostEstimate(
            flops=flops, bytes_accessed=12 * 2**20, transcendentals=8 * 2**20
        ),
    )(
        cond_single, token_mask.reshape(1, toks), w_pair.T, atom_cond, atom_token.reshape(1, atoms),
        atom_mask.reshape(1, atoms), window_start, w_apair.astype(F32).reshape(-1), w_ascale,
        w_ashift, w_aquery, w_akey, w_avalue, w_agate, w_aout, w_update, *large,
    )
    return (tokens_out, atom_update)


def solution(mesh):
    return jax.shard_map(
        functools.partial(shards, mesh.shape["row"]),
        mesh=mesh,
        in_specs=(
            P("groups", "row", None),
            P(("groups", "row"), None),
            P(("groups", "row")),
            P(("groups", "row"), "col", None),
            P(),
            P(),
            P(),
            P(),
            P(None, "col"),
            P(None, "col"),
            P(None, "col"),
            P(None, "col"),
            P("col", None),
            P(("groups", "row", "col"), None),
            P(("groups", "row", "col")),
            P(("groups", "row", "col")),
            P(("groups", "row", "col")),
            P(("groups", "row", "col"), None, None, None),
            P(),
            P(),
            P(),
            P(),
            P(),
            P(),
            P(),
            P(),
            P(),
            P(),
        ),
        out_specs=(P("groups", "row", None), P("groups", None, ("row", "col"))),
        check_vma=False,
    )
```

time: 70 us -> 60.8 us (0.87)
  Pallas kernels: 64.9 us -> 55.4 us
    pallas_call x2 -> x1, Pallas kernels: 64.9 us -> 55.4 us  [shards(): pl.pallas_call(functools.partial(step_kernel, rows), name='sampler_step',...]
    unnamed x34 -> x1, local copies, waits for them, and re-layouts: 3.88 us -> 1.77 us
    pallas_call x0 -> x1, local copies, waits for them, and re-layouts: none -> 1.32 us  [shards(): pl.pallas_call(functools.partial(step_kernel, rows), name='sampler_step',...]
    reshape x2, local copies, waits for them, and re-layouts: 0.18 us -> 1.36 us  [shards(): w_apair.astype(F32).reshape(-1)]
where the time goes in v2:
time: 60.8 us; the launch traced here: 60.5 us
  Pallas kernels  55.4 us (91%)
  local copies, waits for them, and re-layouts  4.45 us (7%)
  between operations  0.64 us (1%)
    pallas_call x1, Pallas kernels, shards(): pl.pallas_call(functools.partial(step_kernel, rows), name='sampler_step',...  55.4 us
    unnamed x1, local copies, waits for them, and re-layouts  1.77 us
    reshape x2, local copies, waits for them, and re-layouts, shards(): w_apair.astype(F32).reshape(-1)  1.36 us
    pallas_call x1, local copies, waits for them, and re-layouts, shards(): pl.pallas_call(functools.partial(step_kernel, rows), name='sampler_step',...  1.32 us

profile of v2, /device:TPU:0, one launch (start us, length us, event | category | flops | bytes accessed | tf_op | source)
XLA Modules:
  0.0 60.5 jit_solution(17960274678765873839)
XLA Ops:
  0.6 0.8 %copy.32 = f32[16,4]{1,0:T(8,128)S(1)} copy(bf16[16,4]{0,1:T(4,128)(2,1)} %param.54) | data formatting | bytes 384 | tf_op jit(solution)/shard_map/reshape | solution.py:492
  1.4 0.6 reshape.24.wap
  2.0 55.4 %sampler_step.1 = (bf16[8,32,768]{2,1,0:T(8,128)(2,1)}, f32[8,3,128]{2,1,0:T(4,128)}) custom-call(bf16[32,768]{1,0:T(8,128)(2,1)} %cond.1, s32[1,32]{1,0:T(1,128)} %bitcast.5, bf16[16,128]{1,0:T(8,128)(2,1)} %bitcast.4, bf16[128,128]{1,0:T(8,128)(2,1)} %acond.1, s32[1,128]{1,0:T(1,128)} %bitcast.6, s32[1,128]{1,0:T(1,128)} %bitcast.7, s32[4]{0:T(128)} %start.1, ...), custom_call_target="tpu_custom_call" | custom-call | flops 4831838208 | bytes 12582912 | tf_op jit(solution)/shard_map/sampler_step/pallas_call | solution.py:440
  57.4 1.3 %copy.33 = f32[8,3,128]{2,0,1:T(8,128)} copy(f32[8,3,128]{2,1,0:T(4,128)} %get-tuple-element.5) | data formatting | bytes 24576 | tf_op jit(solution)/shard_map/sampler_step/pallas_call | solution.py:440
  58.7 1.8 %copy.35 = bf16[8,32,768]{2,1,0:T(8,128)(2,1)} copy(bf16[8,32,768]{2,1,0:T(8,128)(2,1)} %get-tuple-element.8) | data formatting | bytes 786432

commit v3 on v2

--- a/solution.py
+++ b/solution.py
@@ -12,7 +12,6 @@
 AHEAD = 32
 WQ = 32
 WK = 128
-CHUNKS = 2
 F32 = jnp.float32
 BF16 = jnp.bfloat16
 
@@ -49,9 +48,9 @@
     tin_h, wsc_h, wsh_h, pc_h, wq_h, wg_h, wo_h, wog_h, wk_h, wv_h, wta_h, apair_h,
     tout, out,
     tin, wsc, wsh, pc, wq, wg, wo, wog, wk, wv, wta, apair,
-    mx, qb, gate, og, gated, gsib, wosib, pbs, bias, bfull, mk, lk, ac, tk,
+    mx, mstage, qb, gate, og, gtmp, gall, wosib, pbs, bias, bfull, mk, lk, ac, tk,
     asc, ash, pick, windowed, abias,
-    ls, zs, zr, ys, yr, cs, cr, ms, mr, gs, gr, xs, xr,
+    ls, zs, zr, cs, cr, ms, mr, gs, gr, xs, xr,
 ):
     r = lax.axis_index("row")
     c = lax.axis_index("col")
@@ -64,7 +63,8 @@
     i = r // 2
     y = r % 2
     hs = samples // 2
-    ns = hs // CHUNKS
+    per = hs // 2
+    partner = i * 2 + 1 - y
     inv_root = HEAD ** (-0.5)
 
     def wrap(v):
@@ -91,6 +91,7 @@
     for d in range(1, rows):
         greet(wrap(r + d), c)
     greet(r, other)
+    greet(partner, other)
     greet(wrap(r + 2 * c - 1), other)
 
     cond_norm = layer_norm(cond[...]).astype(BF16)
@@ -101,8 +102,8 @@
     scale = jax.nn.sigmoid(dot(cond_norm, wsc[...]))
     shift = dot(cond_norm, wsh[...])
     for s in range(samples):
-        mx[r, s] = (scale * layer_norm(tin[s]) + shift).astype(BF16)
-    pl.semaphore_wait(barrier, rows + 1)
+        mstage[s] = (scale * layer_norm(tin[s]) + shift).astype(BF16)
+    pl.semaphore_wait(barrier, rows + 2)
 
     started = []
 
@@ -111,110 +112,38 @@
         started.append(copy)
         return copy
 
-    def block(row, core, j):
-        return mx.at[row, pl.ds(core * hs + j * ns, ns)]
-
-    steps = [(t, way) for t in range(1, n) for way in (0, 1)]
-    ids = {step: k for k, step in enumerate(steps)}
-    partner = i * 2 + 1 - y
-
-    def valid(step):
-        t, way = step
-        return i >= t if way == 0 else i + t < n
-
-    def line(step):
-        t, way = step
-        return lax.rem(i + n - t, n) if way == 0 else lax.rem(i + t, n)
-
-    def z_copy(j, step):
-        t, way = step
-        back = t - 1
-        src = lax.rem(i + n - back, n) if way == 0 else lax.rem(i + back, n)
-        dest = lax.rem(i + 1, n) if way == 0 else lax.rem(i + n - 1, n)
-        ref = block(src * 2 + y, c, j)
-        k = ids[step]
-        return remote(ref, ref, zs.at[j, k], zr.at[j, k], dest * 2 + y, c)
-
-    def z_sends(step):
-        t, way = step
-        if way == 0:
-            return (i + 1 < n) & (i + 1 >= t)
-        return (i >= 1) & (i + t <= n)
-
-    def y_copy(j, k):
-        src = i if k == 0 else line(steps[k - 1])
-        ref = block(src * 2 + y, c, j)
-        return remote(ref, ref, ys.at[j, k], yr.at[j, k], partner, c)
-
-    def c_copy(j, k, over_y, core):
-        src = i if k == 0 else line(steps[k - 1])
-        col = 1 - y if over_y else y
-        ref = block(src * 2 + col, core, j)
-        slot = len(steps) + k if over_y else k - 1
-        return remote(ref, ref, cs.at[j, slot], cr.at[j, slot], r, other)
-
-    def y_arriving(j, k):
-        src = i if k == 0 else line(steps[k - 1])
-        ref = block(src * 2 + 1 - y, c, j)
-        return remote(ref, ref, ys.at[j, k], yr.at[j, k], partner, c)
-
-    def z_arriving(j, step):
-        ref = block(line(step) * 2 + y, c, j)
-        k = ids[step]
-        return remote(ref, ref, zs.at[j, k], zr.at[j, k], r, other)
-
-    def send_own(j):
-        for way in (0, 1):
-            pl.when(z_sends((1, way)))(lambda: z_copy(j, (1, way)).start())
-        y_copy(j, 0).start()
-
-    def forward_z(j, t):
-        for way in (0, 1):
-            step = (t, way)
-
-            @pl.when(valid(step))
-            def _():
-                z_arriving(j, step).wait_recv()
-                if t + 1 < n:
-                    pl.when(z_sends((t + 1, way)))(lambda: z_copy(j, (t + 1, way)).start())
-                y_copy(j, ids[step] + 1).start()
-                c_copy(j, ids[step] + 1, False, c).start()
-
-    def forward_y(j, t):
-        if t == 0:
-            y_arriving(j, 0).wait_recv()
-            c_copy(j, 0, True, c).start()
-            return
-        for way in (0, 1):
-            step = (t, way)
-
-            @pl.when(valid(step))
-            def _():
-                y_arriving(j, ids[step] + 1).wait_recv()
-                c_copy(j, ids[step] + 1, True, c).start()
-
-    def arrived(j):
-        c_copy(j, 0, True, other).wait_recv()
-        for step in steps:
-
-            @pl.when(valid(step))
-            def _():
-                c_copy(j, ids[step] + 1, False, other).wait_recv()
-                c_copy(j, ids[step] + 1, True, other).wait_recv()
-
-    def all_sent(j):
-        y_copy(j, 0).wait_send()
-        c_copy(j, 0, True, c).wait_send()
-        for step in steps:
-            pl.when(z_sends(step))(lambda: z_copy(j, step).wait_send())
-
-            @pl.when(valid(step))
-            def _():
-                y_copy(j, ids[step] + 1).wait_send()
-                c_copy(j, ids[step] + 1, False, c).wait_send()
-                c_copy(j, ids[step] + 1, True, c).wait_send()
-
-    send_own(0)
+    spots = [(e, w) for e in range(n) for w in (0, 1)][1:]
+
+    def row_at(e, w):
+        return lax.rem(i + n + e, n) * 2 + (1 - y if w else y)
+
+    def send_own(j, k):
+        e, w = spots[k]
+        theirs = (1 - y if w else y) * hs + c * per + j
+        go(
+            remote(
+                mstage.at[theirs], mx.at[r, c * per + j], zs.at[j, k], zr.at[j, k], row_at(e, w), c
+            )
+        )
+
+    def core_copy(j, k, core):
+        e, w = spots[k]
+        ref = mx.at[row_at(-e, w), core * per + j]
+        return remote(ref, ref, cs.at[j, k], cr.at[j, k], r, other)
+
+    def forward(j, k):
+        e, w = spots[k]
+        src = row_at(-e, w)
+        ref = mx.at[src, c * per + j]
+        remote(ref, ref, zs.at[j, k], zr.at[j, k], src, c).wait_recv()
+        go(core_copy(j, k, c))
+
+    far = range(1, len(spots))
+    for j in range(per):
+        send_own(j, 0)
+    for k in far:
+        send_own(0, k)
+    mx[r] = mstage[pl.ds(y * hs, hs)]
 
     placed = (
         lax.broadcasted_iota(jnp.int32, (toks, total), 1)
@@ -240,20 +169,21 @@
         part = dot_nt(wpt[...], pc[q])
         pbs[0, q * heads : (q + 1) * heads] = part[:heads]
         pbs[1, q * heads : (q + 1) * heads] = part[heads:]
-    bias_copy = go(remote(pbs.at[other], bias.at[c], xs.at[5], xr.at[5], r, other))
-    bias[c] = pbs[c]
-    forward_z(0, 1)
-    forward_y(0, 0)
-    send_own(1)
+    bias_copies = [
+        go(remote(pbs.at[other], bias.at[y, c], xs.at[5], xr.at[5], r, other)),
+        go(remote(pbs.at[c], bias.at[y, c], xs.at[8], xr.at[8], partner, c)),
+        go(remote(pbs.at[other], bias.at[y, c], xs.at[9], xr.at[9], partner, other)),
+    ]
+    bias[y, c] = pbs[c]
+    for j in range(per):
+        forward(j, 0)
+    for j in range(1, per):
+        for k in far:
+            send_own(j, k)
 
     for load in loads[4:7]:
         load.wait()
     wide_out = go(remote(wo, wosib, xs.at[0], xr.at[0], r, other))
-    own_rows = mx[r].reshape(samples * toks, width)
-    qb[...] = (dot(own_rows, wq[...]) * inv_root).astype(BF16).astype(F32).reshape(qb.shape)
-    gate[...] = jax.nn.sigmoid(dot(own_rows, wg[...])).reshape(gate.shape)
-    forward_z(0, 2)
-    forward_y(0, 1)
     loads[7].wait()
     og[...] = jax.nn.sigmoid(dot(cond_norm, wog[...]))
 
@@ -279,16 +209,19 @@
     )
     for w in range(windows):
         windowed[w * WK : (w + 1) * WK] = (place == start[w] - base).astype(F32).astype(BF16)
-    for t in range(3, n):
-        forward_z(0, t)
     loads[11].wait()
+    wap_f = wap[...].astype(F32)
     for h in range(AHEADS):
-        acc = apair[:, 0].astype(F32) * wap[h]
+        acc = apair[:, 0].astype(F32) * wap_f[h : h + 1, 0:1]
         for ch in range(1, apair.shape[1]):
-            acc = acc + apair[:, ch].astype(F32) * wap[ch * AHEADS + h]
+            acc = acc + apair[:, ch].astype(F32) * wap_f[h : h + 1, ch : ch + 1]
         abias[:, h * WQ : (h + 1) * WQ] = acc
-    for t in range(2, n):
-        forward_y(0, t)
+
+    for j in range(per):
+        core_copy(j, 0, other).wait_recv()
+    both = mx[pl.ds(2 * i, 2)].reshape(2 * hs * toks, width)
+    qb[...] = (dot(both, wq[...]) * inv_root).astype(BF16).astype(F32).reshape(qb.shape)
+    gate[...] = jax.nn.sigmoid(dot(both, wg[...])).reshape(gate.shape)
 
     columns = wq.shape[1]
     lane = lax.broadcasted_iota(jnp.int32, (heads, columns), 1)
@@ -300,60 +233,54 @@
         keys = dot(keys_in, wk[...]).astype(BF16)
         values = dot(keys_in, wv[...]).astype(BF16)
         values = jnp.concatenate([values, jnp.ones((total, 128), BF16)], axis=1)
-        wide_q = (qb[s][:, None, :] * head_mask[None]).reshape(toks * heads, columns).astype(BF16)
+        wide_q = qb[:, s].reshape(2 * toks, 1, columns) * head_mask[None]
+        wide_q = wide_q.reshape(2 * toks * heads, columns).astype(BF16)
         scores = dot_nt(wide_q, keys) + bfull[...]
         weights = jnp.exp(scores - jnp.max(scores, axis=-1, keepdims=True))
         summed = dot(weights.astype(BF16), values)
         inverse = 1.0 / summed[:, columns:]
         summed = summed[:, :columns] * jnp.concatenate([inverse] * (columns // 128), axis=1)
-        picked = summed.reshape(toks, heads, columns) * head_mask[None]
-        gated[s] = (gate[s] * jnp.sum(picked, axis=1)).astype(BF16)
+        picked = summed.reshape(2 * toks, heads, columns) * head_mask[None]
+        attended = jnp.sum(picked, axis=1).reshape(2, toks, columns)
+        gtmp[:, s] = (gate[:, s] * attended).astype(BF16)
         return carry
 
     for d in range(1, rows):
         slot = mk.at[wrap(r - d)]
         remote(slot, slot, ms.at[d - 1], mr.at[d - 1], r, other).wait_recv()
-    bias_copy.wait_recv()
+    for copy in bias_copies:
+        copy.wait_recv()
     shift_row = (jnp.sum(mk[...], axis=0) - 1.0)[0:1] * 10000.0
-    for k in range(2):
-        cut = slice(k * half, (k + 1) * half)
-        bfull[:, cut] = bias[k] + shift_row[:, cut]
+    for q in range(2):
+        for k in range(2):
+            cut = slice(k * half, (k + 1) * half)
+            tall = slice(q * toks * heads, (q + 1) * toks * heads)
+            bfull[tall, cut] = bias[q, k] + shift_row[:, cut]
     loads[8].wait()
     loads[9].wait()
     gated_copies = []
 
-    def send_gated(j, part):
-        piece = pl.ds(part * hs + j * ns, ns)
-        k = j * 2 + part
-        gated_copies.append(
-            go(remote(gated.at[piece], gsib.at[piece], gs.at[k], gr.at[k], r, other))
-        )
-
-    forward_z(1, 1)
-    forward_y(1, 0)
-    arrived(0)
-    lax.fori_loop(0, ns, attend, None)
-    send_gated(0, 0)
-    forward_z(1, 2)
-    forward_y(1, 1)
-    lax.fori_loop(hs, hs + ns, attend, None)
-    send_gated(0, 1)
-    for t in range(3, n):
-        forward_z(1, t)
-    for t in range(2, n):
-        forward_y(1, t)
-    arrived(1)
-    lax.fori_loop(ns, 2 * ns, attend, None)
-    send_gated(1, 0)
-    lax.fori_loop(hs + ns, hs + 2 * ns, attend, None)
-    send_gated(1, 1)
+    for j in range(per):
+        for k in far:
+            forward(j, k)
+        for k in far:
+            core_copy(j, k, other).wait_recv()
+        lax.fori_loop(0, 2, lambda core, carry: attend(core * per + j, carry), None)
+        for core in range(2):
+            s = core * per + j
+            dst = gall.at[c, y * hs + s]
+            gated_copies.append(go(remote(gtmp.at[1 - y, s], dst, gs.at[0, s], gr.at[0, s], partner, c)))
+            gated_copies.append(go(remote(gtmp.at[1 - y, s], dst, gs.at[1, s], gr.at[1, s], partner, other)))
+            gated_copies.append(go(remote(gtmp.at[y, s], dst, gs.at[2, s], gr.at[2, s], r, other)))
+            gall[c, y * hs + s] = gtmp[y, s]
 
     wide_out.wait_recv()
-    own_part = dot(gated[...].reshape(samples * toks, columns), wo[...])
     loads[10].wait()
     for copy in gated_copies:
         copy.wait_recv()
-    update = own_part + dot(gsib[...].reshape(samples * toks, columns), wosib[...])
+    update = dot(gall[c].reshape(samples * toks, columns), wo[...]) + dot(
+        gall[other].reshape(samples * toks, columns), wosib[...]
+    )
     for s in range(samples):
         tokens = (tin[s].astype(F32) + og[...] * update[s * toks : (s + 1) * toks]).astype(BF16)
         tout[s] = tokens
@@ -364,8 +291,6 @@
         go(remote(mine, lk.at[pl.ds(0, toks)], xs.at[6], xr.at[6], wrap(r + 1), c)),
         go(remote(mine, lk.at[pl.ds(2 * toks, toks)], xs.at[7], xr.at[7], wrap(r - 1), c)),
     ]
-    for j in range(CHUNKS):
-        all_sent(j)
     for copy in started[:-2]:
         copy.wait_send()
     for copy in around:
@@ -407,7 +332,9 @@
             parts.append(picked)
         atom_gated = (head_gate * jnp.concatenate(parts, axis=0)).astype(BF16)
         final = state[edge : edge + atoms] + dot(atom_gated, wao[...])
-        out[s] = dot_nt(wup[...], layer_norm(final).astype(BF16)) * live
+        moved = dot_nt(wup[...], layer_norm(final).astype(BF16)) * live
+        for axis in range(moved.shape[0]):
+            out[axis, s : s + 1] = moved[axis : axis + 1]
     for copy in started[-2:]:
         copy.wait_send()
 
@@ -425,8 +352,8 @@
     heads = w_pair.shape[1] // 2
     columns = w_query.shape[1]
     atoms, da = atom_cond.shape
-    n = rows // 2
-    hops = 2 * (n - 1)
+    hs = samples // 2
+    per = hs // 2
     windows = atoms // WQ
     vmem = pl.BlockSpec(memory_space=pltpu.VMEM)
     smem = pl.BlockSpec(memory_space=pltpu.SMEM)
@@ -442,22 +369,23 @@
         name="sampler_step",
         out_shape=(
             jax.ShapeDtypeStruct((samples, toks, width), BF16),
-            jax.ShapeDtypeStruct((samples, 3, atoms), F32),
+            jax.ShapeDtypeStruct((3, samples, atoms), F32),
         ),
-        in_specs=[vmem] * 6 + [smem] * 2 + [vmem] * 8 + [anywhere] * len(large),
+        in_specs=[vmem] * 6 + [smem] + [vmem] * 9 + [anywhere] * len(large),
         out_specs=[vmem] * 2,
         scratch_shapes=[pltpu.VMEM(a.shape, a.dtype) for a in large]
         + [
-            pltpu.VMEM((rows, samples, toks, width), BF16),
-            pltpu.VMEM((samples, toks, columns), F32),
-            pltpu.VMEM((samples, toks, columns), F32),
+            pltpu.VMEM((rows, hs, toks, width), BF16),
+            pltpu.VMEM((samples, toks, width), BF16),
+            pltpu.VMEM((2, hs, toks, columns), F32),
+            pltpu.VMEM((2, hs, toks, columns), F32),
             pltpu.VMEM((toks, width), F32),
-            pltpu.VMEM((samples, toks, columns), BF16),
-            pltpu.VMEM((samples, toks, columns), BF16),
+            pltpu.VMEM((2, hs, toks, columns), BF16),
+            pltpu.VMEM((2, samples, toks, columns), BF16),
             pltpu.VMEM((columns, width), BF16),
             pltpu.VMEM((2, toks * heads, half), F32),
-            pltpu.VMEM((2, toks * heads, half), F32),
-            pltpu.VMEM((toks * heads, total), F32),
+            pltpu.VMEM((2, 2, toks * heads, half), F32),
+            pltpu.VMEM((2 * toks * heads, total), F32),
             pltpu.VMEM((rows, 8, total), F32),
             pltpu.VMEM((3 * toks, samples * da), BF16),
             pltpu.VMEM((atoms + WK, da), BF16),
@@ -468,18 +396,16 @@
             pltpu.VMEM((windows * WK, atoms + WK), BF16),
             pltpu.VMEM((windows, AHEADS * WQ, WK), F32),
             dma((len(large),)),
-            dma((CHUNKS, hops)),
-            dma((CHUNKS, hops)),
-            dma((CHUNKS, hops + 1)),
-            dma((CHUNKS, hops + 1)),
-            dma((CHUNKS, 2 * hops + 1)),
-            dma((CHUNKS, 2 * hops + 1)),
+            dma((per, rows - 1)),
+            dma((per, rows - 1)),
+            dma((per, rows - 1)),
+            dma((per, rows - 1)),
             dma((rows - 1,)),
             dma((rows - 1,)),
-            dma((2 * CHUNKS,)),
-            dma((2 * CHUNKS,)),
-            dma((8,)),
-            dma((8,)),
+            dma((3, hs)),
+            dma((3, hs)),
+            dma((10,)),
+            dma((10,)),
         ],
         compiler_params=pltpu.CompilerParams(
             collective_id=0, has_side_effects=True, vmem_limit_bytes=56 * 2**20
@@ -489,10 +415,10 @@
         ),
     )(
         cond_single, token_mask.reshape(1, toks), w_pair.T, atom_cond, atom_token.reshape(1, atoms),
-        atom_mask.reshape(1, atoms), window_start, w_apair.astype(F32).reshape(-1), w_ascale,
+        atom_mask.reshape(1, atoms), window_start, w_apair.T, w_ascale,
         w_ashift, w_aquery, w_akey, w_avalue, w_agate, w_aout, w_update, *large,
     )
-    return (tokens_out, atom_update)
+    return (tokens_out, jnp.transpose(atom_update, (1, 0, 2)))
 
 
 def solution(mesh):

time: 60.8 us -> 55.5 us (0.913)
  Pallas kernels: 55.4 us -> 51.4 us
  local copies, waits for them, and re-layouts: 4.45 us -> 3.07 us
    pallas_call x1, Pallas kernels: 55.4 us -> 51.4 us  [shards(): pl.pallas_call(functools.partial(step_kernel, rows), name='sampler_step',...]
    reshape x2 -> x0, local copies, waits for them, and re-layouts: 1.36 us -> none  [shards(): w_apair.astype(F32).reshape(-1)]
    pallas_call x1 -> x0, local copies, waits for them, and re-layouts: 1.32 us -> none  [shards(): pl.pallas_call(functools.partial(step_kernel, rows), name='sampler_step',...]
    unnamed x1 -> x2, local copies, waits for them, and re-layouts: 1.77 us -> 3.07 us
where the time goes in v3:
time: 55.5 us; the launch traced here: 55.2 us
  Pallas kernels  51.4 us (93%)
  local copies, waits for them, and re-layouts  3.07 us (6%)
  between operations  0.65 us (1%)
    pallas_call x1, Pallas kernels, shards(): pl.pallas_call(functools.partial(step_kernel, rows), name='sampler_step',...  51.4 us
    unnamed x2, local copies, waits for them, and re-layouts  3.07 us

profile of v3, /device:TPU:0, one launch (start us, length us, event | category | flops | bytes accessed | tf_op | source)
XLA Modules:
  0.0 55.2 jit_solution(2694645623180164818)
XLA Ops:
  0.6 51.4 %sampler_step.1 = (bf16[8,32,768]{2,1,0:T(8,128)(2,1)}, f32[3,8,128]{2,1,0:T(8,128)}) custom-call(bf16[32,768]{1,0:T(8,128)(2,1)} %cond.1, s32[1,32]{1,0:T(1,128)} %bitcast.9, bf16[16,128]{1,0:T(8,128)(2,1)} %bitcast.7, bf16[128,128]{1,0:T(8,128)(2,1)} %acond.1, s32[1,128]{1,0:T(1,128)} %bitcast.10, s32[1,128]{1,0:T(1,128)} %bitcast.11, s32[4]{0:T(128)} %start.1, ...), custom_call_target="tpu_custom_call" | custom-call | flops 4831838208 | bytes 12582912 | tf_op jit(solution)/shard_map/sampler_step/pallas_call | solution.py:367
  52.1 1.8 %copy.32 = bf16[8,32,768]{2,1,0:T(8,128)(2,1)} copy(bf16[8,32,768]{2,1,0:T(8,128)(2,1)} %get-tuple-element.8) | data formatting | bytes 786432
  53.9 1.3 %copy.33 = f32[8,3,128]{2,0,1:T(8,128)} copy(f32[8,3,128]{2,0,1:T(8,128)} %bitcast.6) | data formatting | bytes 24576

commit v4 on v3

--- a/solution.py
+++ b/solution.py
@@ -101,8 +101,12 @@
         load.start()
     scale = jax.nn.sigmoid(dot(cond_norm, wsc[...]))
     shift = dot(cond_norm, wsh[...])
-    for s in range(samples):
-        mstage[s] = (scale * layer_norm(tin[s]) + shift).astype(BF16)
+
+    def mix(s):
+        return (scale * layer_norm(tin[s]) + shift).astype(BF16)
+
+    for side in range(2):
+        mstage[side * hs + c * per] = mix(side * hs + c * per)
     pl.semaphore_wait(barrier, rows + 2)
 
     started = []
@@ -139,11 +143,16 @@
         go(core_copy(j, k, c))
 
     far = range(1, len(spots))
-    for j in range(per):
-        send_own(j, 0)
+    send_own(0, 0)
     for k in far:
         send_own(0, k)
-    mx[r] = mstage[pl.ds(y * hs, hs)]
+    for j in range(1, per):
+        for side in range(2):
+            mstage[side * hs + c * per + j] = mix(side * hs + c * per + j)
+        send_own(j, 0)
+    for j in range(per):
+        mx[r, c * per + j] = mstage[y * hs + c * per + j]
+        mx[r, other * per + j] = mix(y * hs + other * per + j)
 
     placed = (
         lax.broadcasted_iota(jnp.int32, (toks, total), 1)
@@ -228,7 +237,7 @@
     first = lax.broadcasted_iota(jnp.int32, (heads, columns), 0) * HEAD
     head_mask = ((lane >= first) & (lane < first + HEAD)).astype(F32)
 
-    def attend(s, carry):
+    def attend(s):
         keys_in = mx[:, s].reshape(total, width)
         keys = dot(keys_in, wk[...]).astype(BF16)
         values = dot(keys_in, wv[...]).astype(BF16)
@@ -243,7 +252,6 @@
         picked = summed.reshape(2 * toks, heads, columns) * head_mask[None]
         attended = jnp.sum(picked, axis=1).reshape(2, toks, columns)
         gtmp[:, s] = (gate[:, s] * attended).astype(BF16)
-        return carry
 
     for d in range(1, rows):
         slot = mk.at[wrap(r - d)]
@@ -265,7 +273,8 @@
             forward(j, k)
         for k in far:
             core_copy(j, k, other).wait_recv()
-        lax.fori_loop(0, 2, lambda core, carry: attend(core * per + j, carry), None)
+        for core in range(2):
+            attend(core * per + j)
         for core in range(2):
             s = core * per + j
             dst = gall.at[c, y * hs + s]
@@ -281,11 +290,14 @@
     update = dot(gall[c].reshape(samples * toks, columns), wo[...]) + dot(
         gall[other].reshape(samples * toks, columns), wosib[...]
     )
+    normed = []
     for s in range(samples):
         tokens = (tin[s].astype(F32) + og[...] * update[s * toks : (s + 1) * toks]).astype(BF16)
         tout[s] = tokens
-        proj = dot(layer_norm(tokens).astype(BF16), wta[...]).astype(BF16)
-        lk[toks : 2 * toks, s * da : (s + 1) * da] = proj
+        normed.append(layer_norm(tokens).astype(BF16))
+    proj = dot(jnp.concatenate(normed, axis=0), wta[...]).astype(BF16)
+    for s in range(samples):
+        lk[toks : 2 * toks, s * da : (s + 1) * da] = proj[s * toks : (s + 1) * toks]
     mine = lk.at[pl.ds(toks, toks)]
     around = [
         go(remote(mine, lk.at[pl.ds(0, toks)], xs.at[6], xr.at[6], wrap(r + 1), c)),
@@ -306,35 +318,44 @@
     ones = jnp.ones((WK, da), BF16)
     all_bias = abias[...].reshape(windows * AHEADS * WQ, WK)
     tall = AHEADS * WQ
+    states, mixes = [], []
     for s in range(samples):
         state = atom_cond + looked[:, s * da : (s + 1) * da]
-        mixed = (asc[...] * layer_norm(state) + ash[...]).astype(BF16)
-        kv = dot(mixed, w_kv).astype(BF16)
-        own = dot(mixed[edge : edge + atoms], w_qg)
-        queries = (own[:, :da] * root).astype(BF16).astype(F32)
-        head_gate = jax.nn.sigmoid(own[:, da:])
-        wkv = dot(windowed[...], kv).astype(BF16)
-        scores = []
+        states.append(state[edge : edge + atoms])
+        mixes.append((asc[...] * layer_norm(state) + ash[...]).astype(BF16))
+    kv = dot(jnp.concatenate(mixes, axis=0), w_kv).astype(BF16)
+    own = dot(jnp.concatenate([m[edge : edge + atoms] for m in mixes], axis=0), w_qg)
+    queries = (own[:, :da] * root).astype(BF16).astype(F32)
+    head_gate = jax.nn.sigmoid(own[:, da:])
+    wkv = [dot(windowed[...], kv[s * span : (s + 1) * span]).astype(BF16) for s in range(samples)]
+    scores = []
+    for s in range(samples):
         for w in range(windows):
-            q = queries[w * WQ : (w + 1) * WQ]
+            q = queries[s * atoms + w * WQ : s * atoms + (w + 1) * WQ]
             wide_q = jnp.concatenate([q * m for m in masks], axis=0).astype(BF16)
-            scores.append(dot_nt(wide_q, wkv[w * WK : (w + 1) * WK, :da]))
-        scores = jnp.concatenate(scores, axis=0) + all_bias
-        weights = jnp.exp(scores - jnp.max(scores, axis=-1, keepdims=True)).astype(BF16)
-        parts = []
+            scores.append(
+                dot_nt(wide_q, wkv[s][w * WK : (w + 1) * WK, :da])
+                + all_bias[w * tall : (w + 1) * tall]
+            )
+    weights = [
+        jnp.exp(score - jnp.max(score, axis=-1, keepdims=True)).astype(BF16) for score in scores
+    ]
+    parts = []
+    for s in range(samples):
         for w in range(windows):
-            wide_v = jnp.concatenate([wkv[w * WK : (w + 1) * WK, da:], ones], axis=1)
-            summed = dot(weights[w * tall : (w + 1) * tall], wide_v)
+            wide_v = jnp.concatenate([wkv[s][w * WK : (w + 1) * WK, da:], ones], axis=1)
+            summed = dot(weights[s * windows + w], wide_v)
             summed = summed[:, :da] / summed[:, da:]
             picked = summed[:WQ] * masks[0]
             for h in range(1, AHEADS):
                 picked = picked + summed[h * WQ : (h + 1) * WQ] * masks[h]
             parts.append(picked)
-        atom_gated = (head_gate * jnp.concatenate(parts, axis=0)).astype(BF16)
-        final = state[edge : edge + atoms] + dot(atom_gated, wao[...])
-        moved = dot_nt(wup[...], layer_norm(final).astype(BF16)) * live
+    atom_gated = (head_gate * jnp.concatenate(parts, axis=0)).astype(BF16)
+    final = jnp.concatenate(states, axis=0) + dot(atom_gated, wao[...])
+    moved = dot_nt(wup[...], layer_norm(final).astype(BF16))
+    for s in range(samples):
         for axis in range(moved.shape[0]):
-            out[axis, s : s + 1] = moved[axis : axis + 1]
+            out[axis, s : s + 1] = moved[axis : axis + 1, s * atoms : (s + 1) * atoms] * live
     for copy in started[-2:]:
         copy.wait_send()
 

time: 55.5 us -> 49.3 us (0.89)
  Pallas kernels: 51.4 us -> 45.3 us
    pallas_call x1, Pallas kernels: 51.4 us -> 45.3 us  [shards(): pl.pallas_call(functools.partial(step_kernel, rows), name='sampler_step',...]
where the time goes in v4:
time: 49.3 us; the launch traced here: 49 us
  Pallas kernels  45.3 us (92%)
  local copies, waits for them, and re-layouts  3.07 us (6%)
  between operations  0.65 us (1%)
    pallas_call x1, Pallas kernels, shards(): pl.pallas_call(functools.partial(step_kernel, rows), name='sampler_step',...  45.3 us
    unnamed x2, local copies, waits for them, and re-layouts  3.07 us

profile of v4, /device:TPU:0, one launch (start us, length us, event | category | flops | bytes accessed | tf_op | source)
XLA Modules:
  0.0 49.0 jit_solution(3898451423253324012)
XLA Ops:
  0.6 45.3 %sampler_step.1 = (bf16[8,32,768]{2,1,0:T(8,128)(2,1)}, f32[3,8,128]{2,1,0:T(8,128)}) custom-call(bf16[32,768]{1,0:T(8,128)(2,1)} %cond.1, s32[1,32]{1,0:T(1,128)} %bitcast.9, bf16[16,128]{1,0:T(8,128)(2,1)} %bitcast.7, bf16[128,128]{1,0:T(8,128)(2,1)} %acond.1, s32[1,128]{1,0:T(1,128)} %bitcast.10, s32[1,128]{1,0:T(1,128)} %bitcast.11, s32[4]{0:T(128)} %start.1, ...), custom_call_target="tpu_custom_call" | custom-call | flops 4831838208 | bytes 12582912 | tf_op jit(solution)/shard_map/sampler_step/pallas_call | solution.py:388
  46.0 1.8 %copy.32 = bf16[8,32,768]{2,1,0:T(8,128)(2,1)} copy(bf16[8,32,768]{2,1,0:T(8,128)(2,1)} %get-tuple-element.8) | data formatting | bytes 786432
  47.7 1.3 %copy.33 = f32[8,3,128]{2,0,1:T(8,128)} copy(f32[8,3,128]{2,0,1:T(8,128)} %bitcast.6) | data formatting | bytes 24576
